TPU v7x, 128 devices: a whole 4x4x4 slice. The times are simulated.
128 devices in a mesh: alpha: 16 (over y, x), beta: 8 (over z, core).
Axes of the slice: x: 4, y: 4, z: 4, core: 2. Of those that a mesh axis runs over, the one named last changes fastest.
Arguments:
- coefficients: float32 [16384, 8192], P('alpha', 'beta'), may hold values from -6 to 6
- alpha_energy: float32 [16384], P('alpha'), may hold values from -5 to 5
- beta_energy: float32 [8192], P('beta'), may hold values from -5 to 5
- one_body: float32 [18, 18], replicated, may hold values from -3 to 3
- alpha_source: int32 [128, 3], replicated, may hold values from 0 to 127, as said below
- alpha_pair: int32 [128, 3], replicated, may hold values from 0 to 323
- alpha_links: int32 [128, 3, 128], replicated, may hold values from -128 to 128, as said below
- beta_source: int32 [64, 3], replicated, may hold values from 0 to 63, as said below
- beta_pair: int32 [64, 3], replicated, may hold values from 0 to 323
- beta_links: int32 [64, 3, 128], replicated, may hold values from -128 to 128, as said below
Outputs:
- sigma: float32 [16384, 8192], P('alpha', 'beta')
Inputs may be any that keep to these rules, and one draw needn't show every extreme that they name: `alpha_source`: entry (g, k) names a block that feeds alpha block g. Among the entries of the 8 blocks of one aligned group, at most 2 name blocks of one aligned group of 8 source blocks, and some such pair of groups has exactly 2. `beta_source`: entry (g, k) names a block that feeds beta block g. Among the entries of the 8 blocks of one aligned group, at most 3 name blocks of one aligned group of 8 source blocks, and some such pair of groups has exactly 3. `alpha_links`: 0 where the excitation removes the target string; else the sign times one plus the string's position in the source block. `beta_links`: 0 where the excitation removes the target string; else the sign times one plus the string's position in the source block.
All inputs are finite; a program needn't handle non-finite values.
Results may differ from a plain program's by a relative error of at most 0.0003.
Values sent between devices are 32-bit elements; how exact they have to be, the bound alone decides.
A program may use at most 192 MiB of HBM per device.

v0:
```python
import jax
import jax.numpy as jnp
from jax import lax
from jax.sharding import PartitionSpec as P

SB = 128
ABLK = 8
BBLK = 8
NLA = 3
NLB = 3


def link_matrix(links, pairs, one_body, block_width):
    flat_table = one_body.reshape(-1)
    pair_index = lax.broadcasted_iota(jnp.int32, pairs.shape + (flat_table.shape[0],), pairs.ndim)
    hvalue = jnp.sum(jnp.where(pairs[..., None] == pair_index, flat_table, 0.0), axis=-1)
    sign_value = jnp.sign(links).astype(jnp.float32)
    anchor = jnp.abs(links) - 1
    weights = sign_value * hvalue[..., None]
    strings = lax.broadcasted_iota(jnp.int32, links.shape + (block_width,), links.ndim)
    return jnp.where(anchor[..., None] == strings, weights[..., None], 0.0)


def owner_slots(sources, per_dev, devices, capacity, my_index):
    entries = sources.shape[1]
    owners = sources // per_dev
    belongs = owners == my_index
    slot_rank = jnp.cumsum(belongs.astype(jnp.int32), axis=1) - 1
    levels = lax.broadcasted_iota(jnp.int32, (devices, capacity, entries), 1)
    entry_iota = lax.broadcasted_iota(jnp.int32, (devices, capacity, entries), 2)
    chosen = belongs[:, None, :] & (slot_rank[:, None, :] == levels)
    local_block = jnp.sum(jnp.where(chosen, sources[:, None, :] % per_dev, 0), axis=2)
    entry_index = jnp.sum(jnp.where(chosen, entry_iota, 0), axis=2)
    filled = jnp.any(chosen, axis=2)
    return (local_block.reshape(-1), entry_index.reshape(-1), filled.reshape(-1))


def reader_slots(my_row, per_dev, capacity):
    entries = my_row.shape[0]
    owners = my_row // per_dev
    earlier = lax.broadcasted_iota(jnp.int32, (entries, entries), 1) < lax.broadcasted_iota(
        jnp.int32, (entries, entries), 0
    )
    slot_rank = jnp.sum(((owners[:, None] == owners[None, :]) & earlier).astype(jnp.int32), axis=1)
    return owners * capacity + slot_rank


def on_device(
    coefficients,
    alpha_energy,
    beta_energy,
    one_body,
    alpha_source,
    alpha_pair,
    alpha_links,
    beta_source,
    beta_pair,
    beta_links,
):
    local_rows = coefficients.shape[0]
    local_columns = coefficients.shape[1]
    devices = lax.axis_size("alpha")
    my_alpha = lax.axis_index("alpha")
    entries = ABLK * NLA
    capacity = (entries + devices - 1) // devices
    local_block, entry_index, filled = owner_slots(
        alpha_source.reshape(devices, entries), ABLK, devices, capacity, my_alpha
    )
    blocks_here = coefficients.reshape(ABLK, SB, local_columns)
    picked = jnp.take(blocks_here, local_block, axis=0) * filled.astype(jnp.float32)[:, None, None]
    my_row = lax.dynamic_slice_in_dim(alpha_source, my_alpha * ABLK, ABLK, 0).reshape(entries)
    positions = reader_slots(my_row, ABLK, capacity)
    incoming = lax.all_to_all(
        picked.reshape(devices, capacity, SB, local_columns),
        "alpha",
        split_axis=0,
        concat_axis=0,
        tiled=True,
    )
    source_rows = jnp.take(
        incoming.reshape(devices * capacity, SB, local_columns), positions, axis=0
    )
    my_links = lax.dynamic_slice_in_dim(alpha_links, my_alpha * ABLK, ABLK, 0).reshape(entries, SB)
    my_pairs = lax.dynamic_slice_in_dim(alpha_pair, my_alpha * ABLK, ABLK, 0).reshape(entries)
    matrices = link_matrix(my_links, my_pairs, one_body, SB)
    products = jnp.einsum("eis,esc->eic", matrices, source_rows, precision=lax.Precision.HIGHEST)
    alpha_term = jnp.sum(products.reshape(ABLK, NLA, SB, local_columns), axis=1).reshape(
        local_rows, local_columns
    )
    beta_devices = lax.axis_size("beta")
    my_beta = lax.axis_index("beta")
    beta_entries = BBLK * NLB
    beta_capacity = (beta_entries + beta_devices - 1) // beta_devices
    beta_block, beta_entry, beta_filled = owner_slots(
        beta_source.reshape(beta_devices, beta_entries), BBLK, beta_devices, beta_capacity, my_beta
    )
    columns_here = coefficients.reshape(local_rows, BBLK, SB)
    picked_cols = (
        jnp.take(columns_here, beta_block, axis=1) * beta_filled.astype(jnp.float32)[None, :, None]
    )
    incoming_cols = lax.all_to_all(picked_cols, "beta", split_axis=1, concat_axis=1, tiled=True)
    beta_row = lax.dynamic_slice_in_dim(beta_source, my_beta * BBLK, BBLK, 0).reshape(beta_entries)
    beta_positions = reader_slots(beta_row, BBLK, beta_capacity)
    source_cols = jnp.take(incoming_cols, beta_positions, axis=1)
    my_beta_links = lax.dynamic_slice_in_dim(beta_links, my_beta * BBLK, BBLK, 0).reshape(
        beta_entries, SB
    )
    my_beta_pairs = lax.dynamic_slice_in_dim(beta_pair, my_beta * BBLK, BBLK, 0).reshape(
        beta_entries
    )
    matrices_beta = link_matrix(my_beta_links, my_beta_pairs, one_body, SB)
    coupled = jnp.einsum(
        "res,eis->rei", source_cols, matrices_beta, precision=lax.Precision.HIGHEST
    )
    beta_term = jnp.sum(coupled.reshape(local_rows, BBLK, NLB, SB), axis=2).reshape(
        local_rows, local_columns
    )
    return (alpha_energy[:, None] + beta_energy[None, :]) * coefficients + alpha_term + beta_term


def solution(mesh):
    in_specs = (P("alpha", "beta"), P("alpha"), P("beta"), P(), P(), P(), P(), P(), P(), P())
    out_specs = P("alpha", "beta")
    return jax.shard_map(
        on_device, mesh=mesh, in_specs=in_specs, out_specs=out_specs, check_vma=False
    )
```

profile of v0, /device:TPU:0, one launch (start us, length us, event | category | flops | bytes accessed | tf_op | source)
XLA Modules:
  0.0 477.6 jit_solution(7035975929644803419)
XLA Ops:
  0.0 0.8 copy.73
  0.9 0.2 reduce_window_sum.23
  1.1 0.1 select_reduce_fusion.3
  1.5 0.2 fusion.23
  1.7 5.3 %copy.75 = f32[1024,1024]{0,1:T(8,128)} copy(f32[1024,1024]{1,0:T(8,128)} %param.10) | data formatting | bytes 8388608 | tf_op args[0]
  7.0 5.3 %copy.77 = f32[1024,8,128]{2,0,1:T(8,128)} copy(f32[1024,8,128]{0,2,1:T(8,128)} %bitcast.39) | data formatting | bytes 8388608 | tf_op jit(solution)/shard_map/reshape | solution.py:97
  12.5 9.1 %gather_fusion.2 = f32[24,1024,128]{2,1,0:T(8,128)} fusion(f32[1024,8,128]{2,0,1:T(8,128)} %copy.77, s32[1024]{0:T(1024)S(1)} %pad_clamp_fusion.1), kind=kCustom, calls=%fused_computation.2 | custom fusion | bytes 25165920 | tf_op jit(solution)/shard_map/jit(_take)/gather | solution.py:99
  21.6 11.0 %multiply_bitcast_fusion = f32[1024,24,128]{2,0,1:T(8,128)} fusion(f32[24,1024,128]{2,1,0:T(8,128)} %gather_fusion.2, f32[24]{0:T(128)S(1)} %reshape.676, pred[24]{0:T(512)(128)(4,1)S(1)} %compare_and_fusion), kind=kLoop, calls=%fused_computation.7 | loop fusion | flops 6291456 | bytes 25165944 | tf_op jit(solution)/shard_map/mul | solution.py:99
  32.6 5.7 %all-to-all-start.1 = ((f32[1024,24,128]{2,0,1:T(8,128)}), f32[1024,24,128]{2,0,1:T(8,128)}, u32[]{:S(2)}, u32[]{:S(2)}) async-start(f32[1024,24,128]{2,0,1:T(8,128)} %multiply_bitcast_fusion), calls=%async_computation.1 | async-start | bytes 25165824 | tf_op jit(solution)/shard_map/all_to_all | solution.py:101
  38.2 0.1 copy.64
  38.5 0.2 reduce_window_sum.22
  38.7 0.1 select_reduce_fusion.2
  39.0 0.1 copy.65
  39.1 0.1 fusion.19
  39.3 10.3 %gather_fusion = f32[32,128,1024]{2,1,0:T(8,128)} fusion(f32[8,128,1024]{2,1,0:T(8,128)} %bitcast.34, s32[1024]{0:T(1024)S(1)} %pad_clamp_fusion.3), kind=kCustom, calls=%fused_computation | custom fusion | bytes 33554560 | tf_op jit(solution)/shard_map/jit(_take)/gather | solution.py:70
  49.6 12.5 %select_multiply_fusion = f32[16,2,128,1024]{3,2,1,0:T(8,128)} fusion(f32[16,2,128,1024]{3,2,1,0:T(8,128)} %bitcast.35, f32[16,2]{1,0:T(8,128)S(1)} %copy.67, pred[16,2]{1,0:T(8,128)(4,1)S(1)} %copy.65), kind=kLoop, calls=%fused_computation.4 | loop fusion | flops 8388608 | bytes 33554592 | tf_op jit(solution)/shard_map/mul | solution.py:70
  62.2 115.7 %all-to-all-done.1 = f32[1024,24,128]{2,0,1:T(8,128)} async-done(((f32[1024,24,128]{2,0,1:T(8,128)}), f32[1024,24,128]{2,0,1:T(8,128)}, u32[]{:S(2)}, u32[]{:S(2)}) %all-to-all-start.1) | async-done | bytes 12582944 | tf_op jit(solution)/shard_map/all_to_all | solution.py:101
  177.9 7.1 %all-to-all-start = ((f32[16,2,128,1024]{3,2,1,0:T(8,128)}), f32[16,2,128,1024]{3,2,1,0:T(8,128)}, u32[]{:S(2)}, u32[]{:S(2)}) async-start(f32[16,2,128,1024]{3,2,1,0:T(8,128)} %select_multiply_fusion), calls=%async_computation | async-start | bytes 33554432 | tf_op jit(solution)/shard_map/all_to_all | solution.py:73
  186.3 0.7 abs_add_fusion
  187.0 0.7 abs_add_fusion.1
  187.8 0.2 convert_reduce_fusion
  188.1 0.2 convert_reduce_fusion.1
  188.3 0.2 select_reduce_fusion.1
  188.6 11.6 %gather_fusion.3 = f32[24,1024,128]{2,1,0:T(8,128)} fusion(f32[1024,24,128]{2,0,1:T(8,128)} %all-to-all-done.1, s32[1024]{0:T(1024)S(1)} %pad_clamp_fusion), kind=kCustom, calls=%fused_computation.3 | custom fusion | bytes 25165920 | tf_op jit(solution)/shard_map/jit(_take)/gather | solution.py:104
  200.3 16.4 %fusion = f32[24,128,1024]{2,1,0:T(8,128)} fusion(f32[24,1024,128]{2,1,0:T(8,128)} %gather_fusion.3, pred[24]{0:T(512)(128)(4,1)S(1)} %get-tuple-element.15, f32[24,128]{1,0:T(8,128)S(1)} %broadcast_multiply_fusion, s32[24,128]{1,0:T(8,128)S(1)} %sub.48), kind=kOutput, calls=%fused_computation.5 | convolution fusion | flops 4835770368 | bytes 25190424 | tf_op jit(solution)/shard_map/res,eis->rei/dot_general | solution.py:112
  216.7 8.6 %reduce_sum.85 = f32[1024,8,128]{0,2,1:T(8,128)} reduce(f32[1024,8,3,128]{0,3,2,1:T(8,128)} %bitcast.37, f32[]{:T(128)} %constant.135.clone.1), dimensions={2}, to_apply=%region_11.12 | reduce | flops 2097152 | bytes 16777220 | tf_op jit(solution)/shard_map/reduce_sum | solution.py:115
  225.3 5.4 %copy.80 = f32[1024,1024]{1,0:T(8,128)} copy(f32[1024,1024]{0,1:T(8,128)} %bitcast.38) | data formatting | bytes 8388608 | tf_op jit(solution)/shard_map/reshape | solution.py:115
  230.7 201.5 %all-to-all-done = f32[16,2,128,1024]{3,2,1,0:T(8,128)} async-done(((f32[16,2,128,1024]{3,2,1,0:T(8,128)}), f32[16,2,128,1024]{3,2,1,0:T(8,128)}, u32[]{:S(2)}, u32[]{:S(2)}) %all-to-all-start) | async-done | bytes 16777248 | tf_op jit(solution)/shard_map/all_to_all | solution.py:73
  432.2 12.9 %gather_fusion.1 = f32[24,128,1024]{2,1,0:T(8,128)} fusion(f32[32,128,1024]{2,1,0:T(8,128)} %bitcast.3, s32[1024]{0:T(1024)S(1)} %pad_clamp_fusion.2), kind=kCustom, calls=%fused_computation.1 | custom fusion | bytes 25165920 | tf_op jit(solution)/shard_map/jit(_take)/gather | solution.py:80
  445.1 16.6 %fusion.3 = f32[24,128,1024]{2,1,0:T(8,128)} fusion(f32[24,128,1024]{2,1,0:T(8,128)} %gather_fusion.1, pred[24]{0:T(512)(128)(4,1)S(1)} %get-tuple-element.16, f32[24,128]{1,0:T(8,128)S(1)} %broadcast_multiply_fusion.1, s32[24,128]{1,0:T(8,128)S(1)} %sub.42), kind=kOutput, calls=%fused_computation.9 | convolution fusion | flops 4835770368 | bytes 25190424 | tf_op jit(solution)/shard_map/eis,esc->eic/dot_general | solution.py:86
  461.7 8.6 %reduce_sum.80 = f32[8,128,1024]{2,1,0:T(8,128)} reduce(f32[8,3,128,1024]{3,2,1,0:T(8,128)} %bitcast.36, f32[]{:T(128)} %constant.135.clone.1), dimensions={1}, to_apply=%region_5.6 | reduce | flops 2097152 | bytes 16777220 | tf_op jit(solution)/shard_map/reduce_sum | solution.py:87
  470.2 7.4 %fusion.9 = f32[1024,1024]{1,0:T(8,128)} fusion(f32[1024,1024]{1,0:T(8,128)} %copy.80, f32[8,128,1024]{2,1,0:T(8,128)} %reduce_sum.80, f32[1024,1024]{1,0:T(8,128)} %param.10, f32[1024]{0:T(1024)S(1)} %copy-done.5, f32[1024]{0:T(1024)S(1)} %copy-done.6), kind=kLoop, calls=%fused_computation.16 | loop fusion | flops 4194304 | bytes 16785408 | tf_op jit(solution)/shard_map/add | solution.py:118
  (72 shorter events, 2.5 us)
Async XLA Ops:
  0.0 185.7 %copy-start = (s32[128,3]{0,1:T(4,128)S(1)}, s32[128,3]{0,1:T(4,128)}, u32[]{:S(2)}) copy-start(s32[128,3]{0,1:T(4,128)} %param.15) | copy-start | bytes 4612
  32.6 5.7 %copy-start.4 = (s32[128,3]{0,1:T(4,128)S(1)}, s32[128,3]{0,1:T(4,128)}, u32[]{:S(2)}) copy-start(s32[128,3]{0,1:T(4,128)} %param.14) | copy-start | bytes 4612
  32.6 145.3 %all-to-all-start.1 = ((f32[1024,24,128]{2,0,1:T(8,128)}), f32[1024,24,128]{2,0,1:T(8,128)}, u32[]{:S(2)}, u32[]{:S(2)}) async-start(f32[1024,24,128]{2,0,1:T(8,128)} %multiply_bitcast_fusion), calls=%async_computation.1 | async-start | bytes 25165824 | tf_op jit(solution)/shard_map/all_to_all | solution.py:101
  62.1 122.9 %copy-start.3 = (s32[64,3]{0,1:T(4,128)S(1)}, s32[64,3]{0,1:T(4,128)}, u32[]{:S(2)}) copy-start(s32[64,3]{0,1:T(4,128)} %param.17) | copy-start | bytes 2308
  62.1 123.8 %copy-start.7 = (s32[64,3]{0,1:T(4,128)S(1)}, s32[64,3]{0,1:T(4,128)}, u32[]{:S(2)}) copy-start(s32[64,3]{0,1:T(4,128)} %param.18) | copy-start | bytes 2308
  62.2 124.0 %copy-start.2 = (f32[18,18]{1,0:T(8,128)S(1)}, f32[18,18]{1,0:T(8,128)}, u32[]{:S(2)}) copy-start(f32[18,18]{1,0:T(8,128)} %param.13) | copy-start | bytes 3892
  177.9 254.3 %all-to-all-start = ((f32[16,2,128,1024]{3,2,1,0:T(8,128)}), f32[16,2,128,1024]{3,2,1,0:T(8,128)}, u32[]{:S(2)}, u32[]{:S(2)}) async-start(f32[16,2,128,1024]{3,2,1,0:T(8,128)} %select_multiply_fusion), calls=%async_computation | async-start | bytes 33554432 | tf_op jit(solution)/shard_map/all_to_all | solution.py:73
  461.7 8.6 %copy-start.5 = (f32[1024]{0:T(1024)S(1)}, f32[1024]{0:T(1024)}, u32[]{:S(2)}) copy-start(f32[1024]{0:T(1024)} %param.12) | copy-start | bytes 12292
  461.7 8.6 %copy-start.6 = (f32[1024]{0:T(1024)S(1)}, f32[1024]{0:T(1024)}, u32[]{:S(2)}) copy-start(f32[1024]{0:T(1024)} %param.11) | copy-start | bytes 12292
  461.7 16.0 %copy-start.1 = (s32[128,3]{0,1:T(4,128)S(1)}, s32[128,3]{0,1:T(4,128)}, u32[]{:S(2)}) copy-start(s32[128,3]{0,1:T(4,128)} %param.15) | copy-start | bytes 4612
where the time goes:
time: 478 us
  waiting for transfers between devices  317 us (66%)
  local copies, waits for them, and re-layouts  63.2 us (13%)
  other arithmetic  51.2 us (11%)
  matrix products  33 us (7%)
  starting transfers between devices  12.8 us (3%)
    all_to_all x1, waiting for transfers between devices, on_device(): lax.all_to_all(picked.reshape(devices, capacity, SB, local_columns), 'alp...  202 us
    all_to_all x1, waiting for transfers between devices, on_device(): lax.all_to_all(picked_cols, 'beta', split_axis=1, concat_axis=1, tiled=True)  116 us
    dot_general x1, matrix products, on_device(): jnp.einsum('eis,esc->eic', matrices, source_rows, precision=lax.Precision...  16.6 us
    dot_general x1, matrix products, on_device(): jnp.einsum('res,eis->rei', source_cols, matrices_beta, precision=lax.Prec...  16.4 us
    gather x1, local copies, waits for them, and re-layouts, on_device(): jnp.take(incoming.reshape(devices * capacity, SB, local_columns), positio...  12.9 us
    mul x1, other arithmetic, on_device(): jnp.take(blocks_here, local_block, axis=0)  12.5 us
    gather x1, local copies, waits for them, and re-layouts, on_device(): source_cols = jnp.take(incoming_cols, beta_positions, axis=1)  11.6 us
    mul x1, other arithmetic, on_device(): jnp.take(columns_here, beta_block, axis=1)  11 us
  transfers between devices with their start and end apart: 2, of which 2 were waited for; matrix products, arithmetic and copies ran while one was open for 15% of the time, Pallas kernels for 0%

commit v1 on v0

v1 whole, which is shorter than its diff:
```python
import jax
import jax.numpy as jnp
from jax import lax
from jax.experimental import pallas as pl
from jax.experimental.pallas import tpu as pltpu
from jax.sharding import PartitionSpec as P

MESH = pl.DeviceIdType.MESH
F32, BF16 = jnp.float32, jnp.bfloat16
SB = 128
NCH = 4
NZ = 8


def kernel(
    coef,
    asrc,
    apair,
    alinks,
    bsrc,
    bpair,
    blinks,
    table,
    out,
    gx,
    gy,
    gz,
    stage,
    stage_b,
    split,
    split_b,
    part,
    far,
    near,
    core_out,
    core_in,
    hot,
    hot_b,
    g_send,
    g_recv,
    z_send,
    z_recv,
    r_send,
    r_recv,
    c_send,
    c_recv,
    l_sem,
):
    a = lax.axis_index("alpha")
    b = lax.axis_index("beta")
    y, x, z, core = a // 4, a % 4, b // 2, b % 2

    def step(axis, d):
        s = 1 if d == 0 else 3
        if axis == "x":
            return (y * 4 + (x + s) % 4, b)
        if axis == "y":
            return (((y + s) % 4) * 4 + x, b)
        return (a, ((z + s) % 4) * 2 + core)

    partner = (a, z * 2 + 1 - core)

    def cols(h, c):
        return pl.ds(pl.multiple_of(h * 512 + c * SB, SB), SB)

    axes = ("x", "y")
    bufs = (gx, gy)

    def own(h, c, d):
        return pltpu.make_async_remote_copy(
            src_ref=coef.at[:, cols(h, c)],
            dst_ref=bufs[h].at[2 if d == 0 else 0, c],
            send_sem=g_send.at[h, 0, c, d],
            recv_sem=g_recv.at[h, 0, c, d],
            device_id=step(axes[h], d),
            device_id_type=MESH,
        )

    def relay(h, c, d):
        rows = pl.ds(d * 512, 512)
        return pltpu.make_async_remote_copy(
            src_ref=bufs[h].at[2 if d == 0 else 0, c, rows],
            dst_ref=bufs[h].at[1, c, rows],
            send_sem=g_send.at[h, 1, c, d],
            recv_sem=g_recv.at[h, 1, c, d],
            device_id=step(axes[h], d),
            device_id_type=MESH,
        )

    def own_z(c, d):
        rows = pl.ds(pl.multiple_of(c * SB, SB), SB)
        return pltpu.make_async_remote_copy(
            src_ref=coef.at[rows],
            dst_ref=gz.at[2 if d == 0 else 0, rows],
            send_sem=z_send.at[0, c, d],
            recv_sem=z_recv.at[0, c, d],
            device_id=step("z", d),
            device_id_type=MESH,
        )

    def relay_z(c, d):
        rows = pl.ds(pl.multiple_of(c * SB + d * 64, 64), 64)
        return pltpu.make_async_remote_copy(
            src_ref=gz.at[2 if d == 0 else 0, rows],
            dst_ref=gz.at[1, rows],
            send_sem=z_send.at[1, c, d],
            recv_sem=z_recv.at[1, c, d],
            device_id=step("z", d),
            device_id_type=MESH,
        )

    def send_far(h, c, d):
        return pltpu.make_async_remote_copy(
            src_ref=part.at[h, c, 1, pl.ds(d * 512, 512)],
            dst_ref=far.at[h, c, d],
            send_sem=r_send.at[h, 0, c, d],
            recv_sem=r_recv.at[h, 0, c, d],
            device_id=step(axes[1 - h], d),
            device_id_type=MESH,
        )

    def send_near(h, c, d):
        return pltpu.make_async_remote_copy(
            src_ref=part.at[h, c, 0 if d == 0 else 2],
            dst_ref=near.at[h, c, d],
            send_sem=r_send.at[h, 1, c, d],
            recv_sem=r_recv.at[h, 1, c, d],
            device_id=step(axes[1 - h], d),
            device_id_type=MESH,
        )

    def send_core(c):
        return pltpu.make_async_remote_copy(
            src_ref=core_out.at[c],
            dst_ref=core_in.at[c],
            send_sem=c_send.at[c],
            recv_sem=c_recv.at[c],
            device_id=partner,
            device_id_type=MESH,
        )

    def integral(pair):
        p = pair // 18
        return table[p, pair - p * 18]

    def reader(h, q):
        if h == 0:
            return ((y + q) % 4) * 4 + x
        return y * 4 + (x + q) % 4

    def signed_hot(row):
        s = lax.broadcasted_iota(jnp.int32, (SB, SB), 0)
        return jnp.where(jnp.abs(row) - 1 == s, jnp.where(row > 0, 1.0, -1.0), 0.0)

    def build_alpha(h):
        def body(n, _):
            g = reader(h, n // 8) * 8 + n % 8
            for k in range(3):
                row = alinks[k, pl.ds(g, 1), :]
                hot[h, n * 3 + k] = signed_hot(row).T.astype(BF16)
            return 0

        lax.fori_loop(0, 32, body, 0)

    def build_beta():
        def body(n, _):
            g = (z * 2 + (core + n // 8) % 2) * 8 + n % 8
            for k in range(3):
                row = blinks[k, pl.ds(g, 1), :]
                hot_b[n * 3 + k] = signed_hot(row).astype(BF16)
            return 0

        lax.fori_loop(0, 16, body, 0)

    def pieces(v):
        hi = v.astype(BF16)
        return hi, (v - hi.astype(F32)).astype(BF16)

    def compute_alpha(h, c):
        copies = [pltpu.make_async_copy(coef.at[:, cols(h, c)], stage.at[0], l_sem.at[0])]
        for q in range(3):
            copies.append(
                pltpu.make_async_copy(bufs[h].at[q, c], stage.at[q + 1], l_sem.at[q + 1])
            )
        for cp in copies:
            cp.start()
        for cp in copies:
            cp.wait()

        def split_body(n, _):
            rows = pl.ds(pl.multiple_of((n % 8) * SB, SB), SB)
            hi, lo = pieces(stage[n // 8, rows, :])
            split[n, 0:SB, :] = hi
            split[n, SB : 2 * SB, :] = lo
            return 0

        lax.fori_loop(0, 32, split_body, 0, unroll=2)

        def target(n):
            g = reader(h, n // 8) * 8 + n % 8
            acc = jnp.zeros((SB, SB), F32)
            for k in range(3):
                src = asrc[k, g]
                sy, sx = (src >> 5) & 3, (src >> 3) & 3
                if h == 0:
                    here, q = sy == y, (sx - x) & 3
                else:
                    here, q = sx == x, (sy - y) & 3
                weight = jnp.where(here, integral(apair[k, g]), 0.0)
                w = hot[h, n * 3 + k]
                acc += weight * jnp.dot(
                    jnp.concatenate([w, w], axis=1),
                    split[q * 8 + (src & 7)],
                    preferred_element_type=F32,
                )
            return acc

        def mine(n, _):
            rows = pl.ds(pl.multiple_of(n * SB, SB), SB)
            out[rows, cols(h, c)] += target(n)
            return 0

        lax.fori_loop(0, 8, mine, 0, unroll=4)

        def others(n, _):
            rows = pl.ds(pl.multiple_of((n % 8) * SB, SB), SB)
            part[h, c, n // 8 - 1, rows, :] = target(n)
            return 0

        lax.fori_loop(8, 32, others, 0, unroll=4)

    def compute_beta(c):
        rows = pl.ds(pl.multiple_of(c * SB, SB), SB)
        copies = [pltpu.make_async_copy(coef.at[rows], stage_b.at[0], l_sem.at[4])]
        for q in range(3):
            copies.append(
                pltpu.make_async_copy(gz.at[q, rows], stage_b.at[q + 1], l_sem.at[q + 5])
            )
        for cp in copies:
            cp.start()
        for cp in copies:
            cp.wait()

        def split_body(n, _):
            hi, lo = pieces(stage_b[n // 8, :, pl.ds(pl.multiple_of((n % 8) * SB, SB), SB)])
            split_b[n, :, 0:SB] = hi
            split_b[n, :, SB : 2 * SB] = lo
            return 0

        lax.fori_loop(0, 32, split_body, 0, unroll=2)

        def target(n):
            g = (z * 2 + (core + n // 8) % 2) * 8 + n % 8
            acc = jnp.zeros((SB, SB), F32)
            for k in range(3):
                src = bsrc[k, g]
                sz, sc = (src >> 4) & 3, (src >> 3) & 1
                weight = jnp.where(sc == core, integral(bpair[k, g]), 0.0)
                w = hot_b[n * 3 + k]
                acc += weight * jnp.dot(
                    split_b[((sz - z) & 3) * 8 + (src & 7)],
                    jnp.concatenate([w, w], axis=0),
                    preferred_element_type=F32,
                )
            return acc

        def mine(n, _):
            at = pl.ds(pl.multiple_of(n * SB, SB), SB)
            out[rows, at] += target(n)
            return 0

        lax.fori_loop(0, 8, mine, 0, unroll=4)

        def others(n, _):
            at = pl.ds(pl.multiple_of((n - 8) * SB, SB), SB)
            core_out[c, :, at] = target(n)
            return 0

        lax.fori_loop(8, 16, others, 0, unroll=4)

    def pass_on(h, c):
        for d in range(2):
            send_far(h, c, d).wait_recv()
            slot = 0 if d == 0 else 2

            def body(n, _):
                rows = pl.ds(pl.multiple_of(d * 512 + n * SB, SB), SB)
                part[h, c, slot, rows, :] += far[h, c, d, pl.ds(pl.multiple_of(n * SB, SB), SB), :]
                return 0

            lax.fori_loop(0, 4, body, 0)
            send_near(h, c, d).start()

    def finish(h, c):
        for d in range(2):
            send_near(h, c, d).wait_recv()

        def body(n, _):
            rows = pl.ds(pl.multiple_of(n * SB, SB), SB)
            out[rows, cols(h, c)] += near[h, c, 0, rows, :] + near[h, c, 1, rows, :]
            return 0

        lax.fori_loop(0, 8, body, 0)

    def finish_core(c):
        send_core(c).wait_recv()
        rows = pl.ds(pl.multiple_of(c * SB, SB), SB)
        out[rows, :] += core_in[c]

    barrier = pltpu.get_barrier_semaphore()
    for axis in ("x", "y", "z"):
        for d in range(2):
            pl.semaphore_signal(barrier, inc=1, device_id=step(axis, d), device_id_type=MESH)
    pl.semaphore_signal(barrier, inc=1, device_id=partner, device_id_type=MESH)
    pl.semaphore_wait(barrier, 7)

    for c in range(2):
        for d in range(2):
            own(0, c, d).start()
            own(1, c, d).start()
            own_z(c, d).start()

    out[...] = jnp.zeros_like(out)
    build_alpha(0)

    def move_on(c):
        for h in range(2):
            for d in range(2):
                own(h, c, d).wait_recv()
                relay(h, c, d).start()

        @pl.when(c < NCH - 2)
        def _():
            for h in range(2):
                for d in range(2):
                    own(h, c + 2, d).start()

    def move_on_z(c):
        for d in range(2):
            own_z(c, d).wait_recv()
            relay_z(c, d).start()

        @pl.when(c < NZ - 2)
        def _():
            for d in range(2):
                own_z(c + 2, d).start()

    move_on(0)
    move_on_z(0)
    build_alpha(1)
    build_beta()

    def loop(t, _):
        @pl.when(t < NCH - 1)
        def _():
            move_on(t + 1)

        @pl.when(t < NZ - 1)
        def _():
            move_on_z(t + 1)

        @pl.when(t < NCH)
        def _():
            for h in range(2):
                for d in range(2):
                    relay(h, t, d).wait_recv()
                compute_alpha(h, t)

        @pl.when(t == 2)
        def _():
            for c in range(2):
                for h in range(2):
                    for d in range(2):
                        send_far(h, c, d).start()

        @pl.when((t >= 2) & (t < NCH))
        def _():
            for h in range(2):
                for d in range(2):
                    send_far(h, t, d).start()

        @pl.when((t >= 3) & (t < 7))
        def _():
            for h in range(2):
                pass_on(h, t - 3)

        for d in range(2):
            relay_z(t, d).wait_recv()
        compute_beta(t)
        send_core(t).start()

        @pl.when(t >= 6)
        def _():
            for h in range(2):
                finish(h, t - 6)

        @pl.when(t >= 1)
        def _():
            finish_core(t - 1)

        return 0

    lax.fori_loop(0, NZ, loop, 0)
    finish_core(NZ - 1)

    def last(c, _):
        for h in range(2):
            finish(h, c)
        return 0

    lax.fori_loop(2, NCH, last, 0)

    def drain(c, _):
        for h in range(2):
            for d in range(2):
                own(h, c, d).wait_send()
                relay(h, c, d).wait_send()
                send_far(h, c, d).wait_send()
                send_near(h, c, d).wait_send()
        return 0

    lax.fori_loop(0, NCH, drain, 0)

    def drain_z(c, _):
        for d in range(2):
            own_z(c, d).wait_send()
            relay_z(c, d).wait_send()
        send_core(c).wait_send()
        return 0

    lax.fori_loop(0, NZ, drain_z, 0)


def couplings(coef, one_body, asrc, apair, alinks, bsrc, bpair, blinks):
    hbm = pl.BlockSpec(memory_space=pl.ANY)
    vmem = pl.BlockSpec(memory_space=pltpu.VMEM)
    smem = pl.BlockSpec(memory_space=pltpu.SMEM)
    dma = pltpu.SemaphoreType.DMA
    return pl.pallas_call(
        kernel,
        out_shape=[
            jax.ShapeDtypeStruct((1024, 1024), F32),
            jax.ShapeDtypeStruct((3, NCH, 1024, SB), F32),
            jax.ShapeDtypeStruct((3, NCH, 1024, SB), F32),
            jax.ShapeDtypeStruct((3, 1024, 1024), F32),
        ],
        in_specs=[hbm, smem, smem, vmem, smem, smem, vmem, smem],
        out_specs=[vmem, hbm, hbm, hbm],
        scratch_shapes=[
            pltpu.VMEM((4, 1024, SB), F32),
            pltpu.VMEM((4, SB, 1024), F32),
            pltpu.VMEM((32, 2 * SB, SB), BF16),
            pltpu.VMEM((32, SB, 2 * SB), BF16),
            pltpu.VMEM((2, NCH, 3, 1024, SB), F32),
            pltpu.VMEM((2, NCH, 2, 512, SB), F32),
            pltpu.VMEM((2, NCH, 2, 1024, SB), F32),
            pltpu.VMEM((NZ, SB, 1024), F32),
            pltpu.VMEM((NZ, SB, 1024), F32),
            pltpu.VMEM((2, 96, SB, SB), BF16),
            pltpu.VMEM((48, SB, SB), BF16),
            dma((2, 2, NCH, 2)),
            dma((2, 2, NCH, 2)),
            dma((2, NZ, 2)),
            dma((2, NZ, 2)),
            dma((2, 2, NCH, 2)),
            dma((2, 2, NCH, 2)),
            dma((NZ,)),
            dma((NZ,)),
            dma((8,)),
        ],
        compiler_params=pltpu.CompilerParams(
            collective_id=0, has_side_effects=True, vmem_limit_bytes=60 * 2**20
        ),
        name="couplings",
    )(coef, asrc, apair, alinks, bsrc, bpair, blinks, one_body)[0]


def on_device(
    coefficients,
    alpha_energy,
    beta_energy,
    one_body,
    alpha_source,
    alpha_pair,
    alpha_links,
    beta_source,
    beta_pair,
    beta_links,
):
    terms = couplings(
        coefficients,
        one_body,
        alpha_source.T,
        alpha_pair.T,
        alpha_links.transpose(1, 0, 2),
        beta_source.T,
        beta_pair.T,
        beta_links.transpose(1, 0, 2),
    )
    return (alpha_energy[:, None] + beta_energy[None, :]) * coefficients + terms


def solution(mesh):
    in_specs = (P("alpha", "beta"), P("alpha"), P("beta"), P(), P(), P(), P(), P(), P(), P())
    out_specs = P("alpha", "beta")
    return jax.shard_map(
        on_device, mesh=mesh, in_specs=in_specs, out_specs=out_specs, check_vma=False
    )
```

time: 478 us -> 162 us (0.34)
  waiting for transfers between devices: 317 us -> 0 us
  Pallas kernels: 0 us -> 155 us
  local copies, waits for them, and re-layouts: 63.2 us -> 0.01 us
  other arithmetic: 51.2 us -> 6.02 us
  matrix products: 33 us -> 0 us
  starting transfers between devices: 12.8 us -> 0 us
    all_to_all x2 -> x0, waiting for transfers between devices: 317 us -> none  [the longest x1 202 us: on_device(): lax.all_to_all(picked.reshape(devices, capacity, SB, local_columns), 'alp...]
    pallas_call x0 -> x1, Pallas kernels: none -> 155 us  [couplings(): pl.pallas_call(kernel, out_shape=[jax.ShapeDtypeStruct((1024, 1024), F32)...]
    gather x4 -> x0, local copies, waits for them, and re-layouts: 44 us -> none  [the longest x1 12.9 us: on_device(): jnp.take(incoming.reshape(devices * capacity, SB, local_columns), positio...]
    dot_general x2 -> x0, matrix products: 33 us -> none  [the longest x1 16.6 us: on_device(): jnp.einsum('eis,esc->eic', matrices, source_rows, precision=lax.Precision...]
    mul x4 -> x0, other arithmetic: 23.6 us -> none  [the longest x1 12.5 us: on_device(): jnp.take(blocks_here, local_block, axis=0)]
    reduce_sum x7 -> x0, other arithmetic: 18 us -> none  [the longest x1 8.6 us: on_device(): jnp.sum(coupled.reshape(local_rows, BBLK, NLB, SB), axis=2)]
    all_to_all x2 -> x0, starting transfers between devices: 12.8 us -> none  [the longest x1 7.1 us: on_device(): lax.all_to_all(picked.reshape(devices, capacity, SB, local_columns), 'alp...]
    reshape x12 -> x0, local copies, waits for them, and re-layouts: 11.5 us -> none  [the longest x1 5.39 us: on_device(): jnp.sum(coupled.reshape(local_rows, BBLK, NLB, SB), axis=2)]
  transfers between devices with their start and end apart: 2 -> 0, of which waited for: 2 -> 0; matrix products, arithmetic and copies ran while one was open for 15% -> 0% of each run, Pallas kernels for 0% -> 0%
where the time goes in v1:
time: 162 us; the launch traced here: 161 us
  Pallas kernels  155 us (96%)
  other arithmetic  6.02 us (4%)
    pallas_call x1, Pallas kernels, couplings(): pl.pallas_call(kernel, out_shape=[jax.ShapeDtypeStruct((1024, 1024), F32)...  155 us
    add x1, other arithmetic, on_device(): return (alpha_energy[:, None] + beta_energy[None, :]) * coefficients + terms  6.02 us

profile of v1, /device:TPU:0, one launch (start us, length us, event | category | flops | bytes accessed | tf_op | source)
XLA Modules:
  0.0 161.2 jit_solution(4535057865757825028)
XLA Ops:
  0.0 0.0 copy-start
  0.0 0.0 copy-start.1
  0.0 155.1 %couplings.1 = (f32[1024,1024]{1,0:T(8,128)}, f32[3,4,1024,128]{3,2,1,0:T(8,128)}, f32[3,4,1024,128]{3,2,1,0:T(8,128)}, f32[3,1024,1024]{2,1,0:T(8,128)}) custom-call(f32[1024,1024]{1,0:T(8,128)} %coef.1, s32[3,128]{1,0:T(4,128)} %bitcast.8, s32[3,128]{1,0:T(4,128)} %bitcast.9, s32[3,128,128]{2,1,0:T(8,128)} %bitcast.6, s32[3,64]{1,0:T(4,128)} %bitcast.10, ...), custom_call_target="tpu_custom_call" | custom-call | tf_op jit(solution)/shard_map/couplings/pallas_call | solution.py:439
  155.1 0.0 copy-done
  155.1 0.0 copy-done.1
  155.2 6.0 %multiply_add_fusion = f32[1024,1024]{1,0:T(8,128)} fusion(f32[1024,1024]{1,0:T(8,128)} %get-tuple-element.6, f32[1024,1024]{1,0:T(8,128)} %coef.1, f32[1024]{0:T(1024)S(1)} %copy-done, f32[1024]{0:T(1024)S(1)} %copy-done.1), kind=kLoop, calls=%fused_computation | loop fusion | flops 3145728 | bytes 12591104 | tf_op jit(solution)/shard_map/add | solution.py:500
Async XLA Ops:
  0.0 155.1 %copy-start = (f32[1024]{0:T(1024)S(1)}, f32[1024]{0:T(1024)}, u32[]{:S(2)}) copy-start(f32[1024]{0:T(1024)} %param.12) | copy-start | bytes 12292
  0.0 155.1 %copy-start.1 = (f32[1024]{0:T(1024)S(1)}, f32[1024]{0:T(1024)}, u32[]{:S(2)}) copy-start(f32[1024]{0:T(1024)} %param.11) | copy-start | bytes 12292

commit v2 on v1

--- a/solution.py
+++ b/solution.py
@@ -1,3 +1,5 @@
+import numpy as np
+
 import jax
 import jax.numpy as jnp
 from jax import lax
@@ -10,9 +12,595 @@
 SB = 128
 NCH = 4
 NZ = 8
-
-
-def kernel(
+SLOTS = 13
+
+LINK = (1, 3, 4, 12)
+
+
+def link_of(o, i):
+    return (o + i) % 4
+
+
+def spans(links):
+    found = [0]
+    for link in links:
+        found = found + [v ^ LINK[link] for v in found]
+    return found
+
+
+def reader_masks(o):
+    last, third = LINK[link_of(o, 3)], LINK[link_of(o, 2)]
+    return (0, last, third, third ^ last)
+
+
+HOT_SLOT = {m: i for i, m in enumerate(sorted({m for o in range(4) for m in reader_masks(o)}))}
+
+
+def message_masks():
+    shape = (4, 16, 16)
+    two_readers, two_sources = np.zeros(shape, np.float32), np.zeros(shape, np.float32)
+    three_sources, three_readers = np.zeros(shape, np.float32), np.zeros(shape, np.float32)
+    for o in range(4):
+        l1, l2, l3, l4 = (link_of(o, i) for i in range(4))
+        for n in range(16):
+            for v in spans((l3, l4)):
+                two_readers[o, n, n ^ LINK[l2] ^ v] = 1
+            for v in spans((l1,)):
+                two_sources[o, n, n ^ v] = 1
+            for v in spans((l1, l2)):
+                three_sources[o, n, n ^ v] = 1
+            for v in spans((l4,)):
+                three_readers[o, n, n ^ LINK[l3] ^ v] = 1
+    return two_readers, two_sources, three_sources, three_readers
+
+
+def rows_of_device():
+    pick = np.zeros((16, 2, 2, 4, 4, 16), np.float32)
+    for n in range(16):
+        for stage in range(2):
+            for o in range(4):
+                pick[n, stage, 0, o, o, n] = 1
+                pick[n, stage, 1, o, o, n ^ LINK[link_of(o, stage + 1)]] = 1
+    return pick.reshape(16, 2, 8, 64)
+
+
+def message_tables(source, me):
+    two_readers, two_sources, three_sources, three_readers = (
+        jnp.asarray(m.reshape(64, 16)) for m in message_masks()
+    )
+    blocks = jnp.arange(128, dtype=jnp.int32)
+    by_reader = source.reshape(16, 24)
+    named = jnp.any(by_reader[:, :, None] == blocks, axis=1).astype(F32)
+    devices = jnp.arange(16, dtype=jnp.int32)
+    fed = jnp.any((source >> 3)[:, :, None] == devices, axis=1).astype(F32)
+    two = (jnp.dot(two_readers, named) > 0.5) & (jnp.repeat(two_sources, 8, axis=1) > 0.5)
+    three = (jnp.dot(three_sources, fed.T) > 0.5) & (jnp.repeat(three_readers, 8, axis=1) > 0.5)
+    masks = jnp.stack([two, three]).astype(F32)
+    most = jnp.max(jnp.sum(masks, axis=2))
+    pick = lax.dynamic_index_in_dim(jnp.asarray(rows_of_device()), me, 0, keepdims=False)
+    mine = jnp.einsum("trm,tmb->trb", pick, masks)
+    before = jnp.asarray(np.triu(np.ones((128, 128), np.float32), 1))
+    rank = jnp.einsum("trb,bc->trc", mine, before).astype(jnp.int32)
+    here = mine > 0.5
+    slots = jnp.arange(16, dtype=jnp.int32)
+    chosen = here[:, :4, None, :] & (rank[:, :4, None, :] == slots[:, None])
+    sent = jnp.sum(jnp.where(chosen, blocks, 0), axis=3)
+    got = jnp.where(here[:, 4:], jnp.minimum(rank[:, 4:], SLOTS - 1), -1)
+    return sent, got, most
+
+
+def named_kernel(
+    coef,
+    asrc,
+    apair,
+    alinks_hbm,
+    bsrc,
+    bpair,
+    blinks_hbm,
+    table,
+    sent,
+    got,
+    out_hbm,
+    got1,
+    got2,
+    gz,
+    gc,
+    gf,
+    got_b,
+    out,
+    alinks,
+    blinks,
+    stage,
+    split,
+    held,
+    pack,
+    part3,
+    *rest,
+):
+    got3, rest = rest[:8], rest[8:]
+    part4, got4, stage_b, split_b, part_b, hot, hot_b, s_sem, r_sem, zs_sem, zr_sem, l_sem = rest
+    a = lax.axis_index("alpha")
+    b = lax.axis_index("beta")
+    y, x, z, core = a // 4, a % 4, b // 2, b % 2
+
+    def over(place, link):
+        py, px = place
+        if link == 0:
+            return (py, px + 1 - 2 * (px % 2))
+        if link == 1:
+            return (py, 3 - px)
+        if link == 2:
+            return (py + 1 - 2 * (py % 2), px)
+        return (3 - py, px)
+
+    def index(place):
+        return place[0] * 4 + place[1]
+
+    def peer(link):
+        return (index(over((y, x), link)), b)
+
+    def over_z(pair):
+        return z + 1 - 2 * (z % 2) if pair == 0 else 3 - z
+
+    partner = (a, z * 2 + 1 - core)
+
+    def choose(o, values):
+        return jnp.where(
+            o == 0, values[0], jnp.where(o == 1, values[1], jnp.where(o == 2, values[2], values[3]))
+        )
+
+    def each(o, act):
+        for k in range(4):
+
+            @pl.when(o == k)
+            def _(k=k):
+                act(k)
+
+    def columns(w, o):
+        return pl.ds(pl.multiple_of((w * 4 + o) * SB, SB), SB)
+
+    def block(n):
+        return pl.ds(pl.multiple_of(n * SB, SB), SB)
+
+    def send(i, w, o):
+        ch = w * 4 + o
+        src = (coef.at[:, :, columns(w, o)], pack.at[ch], part3.at[ch], part4.at[ch])[i]
+        dst = got3[ch] if i == 2 else (got1, got2, None, got4)[i].at[ch]
+        return pltpu.make_async_remote_copy(
+            src_ref=src,
+            dst_ref=dst,
+            send_sem=s_sem.at[i, ch],
+            recv_sem=r_sem.at[i, ch],
+            device_id=peer(link_of(o, i)),
+            device_id_type=MESH,
+        )
+
+    def blocks_b(h, c):
+        return pl.ds(h * 4 + c * 2, 2)
+
+    def send_z(h, c):
+        return pltpu.make_async_remote_copy(
+            src_ref=coef.at[blocks_b(h, c)],
+            dst_ref=gz.at[blocks_b(h, c)],
+            send_sem=zs_sem.at[0, h, c],
+            recv_sem=zr_sem.at[0, h, c],
+            device_id=(a, over_z(h) * 2 + core),
+            device_id_type=MESH,
+        )
+
+    def send_c(h, c):
+        return pltpu.make_async_remote_copy(
+            src_ref=coef.at[blocks_b(h, c)],
+            dst_ref=gc.at[blocks_b(h, c)],
+            send_sem=zs_sem.at[1, h, c],
+            recv_sem=zr_sem.at[1, h, c],
+            device_id=partner,
+            device_id_type=MESH,
+        )
+
+    def send_f(h, c):
+        return pltpu.make_async_remote_copy(
+            src_ref=gz.at[blocks_b(h, c)],
+            dst_ref=gf.at[blocks_b(h, c)],
+            send_sem=zs_sem.at[2, h, c],
+            recv_sem=zr_sem.at[2, h, c],
+            device_id=partner,
+            device_id_type=MESH,
+        )
+
+    def send_b(h, c):
+        return pltpu.make_async_remote_copy(
+            src_ref=part_b.at[h, c],
+            dst_ref=got_b.at[blocks_b(h, c)],
+            send_sem=zs_sem.at[3, h, c],
+            recv_sem=zr_sem.at[3, h, c],
+            device_id=(a, over_z(1 - h) * 2 + core),
+            device_id_type=MESH,
+        )
+
+    def integral(pair):
+        p = pair // 18
+        return table[p, pair - p * 18]
+
+    def signed_hot(row):
+        s = lax.broadcasted_iota(jnp.int32, (SB, SB), 0)
+        return jnp.where(jnp.abs(row) - 1 == s, jnp.where(row > 0, 1.0, -1.0), 0.0)
+
+    def pieces(v):
+        hi = v.astype(BF16)
+        return hi, (v - hi.astype(F32)).astype(BF16)
+
+    def build_alpha():
+        for mask, slot in HOT_SLOT.items():
+            place = (y, x)
+            for link in range(4):
+                if mask & 3 == LINK[link] or mask & 12 == LINK[link]:
+                    place = over(place, link)
+            if mask & 3 == 2:
+                place = over(over(place, 0), 1)
+            if mask & 12 == 8:
+                place = over(over(place, 2), 3)
+            reader = index(place)
+
+            def body(n, _, slot=slot, reader=reader):
+                for k in range(3):
+                    row = alinks[k, pl.ds(reader * 8 + n, 1), :]
+                    hot[slot, n * 3 + k] = signed_hot(row).T.astype(BF16)
+                return 0
+
+            lax.fori_loop(0, 8, body, 0, unroll=4)
+
+    def build_beta():
+        for slot in range(3):
+            reader = (z if slot == 0 else over_z(slot - 1)) * 2 + core
+
+            def body(n, _, slot=slot, reader=reader):
+                for k in range(3):
+                    row = blinks[k, pl.ds(reader * 8 + n, 1), :]
+                    hot_b[slot, n * 3 + k] = signed_hot(row).astype(BF16)
+                return 0
+
+            lax.fori_loop(0, 8, body, 0, unroll=4)
+
+    def load(w, o, buf, second):
+        copies = [
+            pltpu.make_async_copy(
+                coef.at[:, :, columns(w, o)], stage.at[buf, pl.ds(0, 8)], l_sem.at[buf, 0]
+            ),
+            pltpu.make_async_copy(
+                got1.at[w * 4 + o], stage.at[buf, pl.ds(8, 8)], l_sem.at[buf, 1]
+            ),
+        ]
+        if second:
+            copies.append(
+                pltpu.make_async_copy(
+                    got2.at[w * 4 + o], stage.at[buf, pl.ds(16, SLOTS)], l_sem.at[buf, 2]
+                )
+            )
+        return copies
+
+    def start_load(w, o, second):
+        for cp in load(w, o, o % 2, second):
+            cp.start()
+
+    def wait_load(w, o, second):
+        for cp in load(w, o, o % 2, second):
+            cp.wait()
+
+    def ready(w, o, i):
+        def first(k):
+            if k == 0:
+                send(i, w, 0).wait_recv()
+                start_load(w, 0, i == 1)
+            if k < 3:
+                send(i, w, k + 1).wait_recv()
+                start_load(w, k + 1, i == 1)
+            wait_load(w, k, i == 1)
+
+        each(o, first)
+
+    def second_exchange(w):
+        def body(o, _):
+            ready(w, o, 0)
+            buf = o % 2
+
+            def hold(n, _):
+                held[n] = stage[buf, n]
+                return 0
+
+            lax.fori_loop(0, 16, hold, 0, unroll=4)
+
+            def fill(s, _):
+                wanted = sent[0, o, s]
+                at = jnp.where((wanted >> 3) == a, 0, 8) + (wanted & 7)
+                pack[w * 4 + o, s] = held[at]
+                return 0
+
+            lax.fori_loop(0, SLOTS, fill, 0)
+            each(o, lambda k: send(1, w, k).start())
+            return 0
+
+        lax.fori_loop(0, 4, body, 0)
+
+    def third_exchange(w):
+        def body(o, _):
+            ready(w, o, 1)
+            buf = o % 2
+            ch = w * 4 + o
+            m1 = choose(o, [LINK[link_of(k, 0)] for k in range(4)])
+            m2 = choose(o, [LINK[link_of(k, 1)] for k in range(4)])
+            m3 = choose(o, [LINK[link_of(k, 2)] for k in range(4)])
+            hots = [
+                choose(o, [HOT_SLOT[reader_masks(k)[role]] for k in range(4)]) for role in range(4)
+            ]
+
+            def split_body(n, _):
+                hi, lo = pieces(stage[buf, n])
+                split[n, 0:SB, :] = hi
+                split[n, SB : 2 * SB, :] = lo
+                return 0
+
+            lax.fori_loop(0, 16 + SLOTS, split_body, 0, unroll=8)
+
+            def target(g, slot):
+                acc = jnp.zeros((SB, SB), F32)
+                for k in range(3):
+                    src = asrc[k, g]
+                    apart = (src >> 3) ^ a
+                    inner = src & 7
+                    over_two = (apart == m2) | (apart == (m1 ^ m2))
+                    here = over_two | (apart == 0) | (apart == m1)
+                    arrived = 16 + jnp.maximum(got[0, o, src], 0)
+                    at = jnp.where(over_two, arrived, jnp.where(apart == m1, 8 + inner, inner))
+                    weight = jnp.where(here, integral(apair[k, g]), 0.0)
+                    w_k = hot[slot, (g & 7) * 3 + k]
+                    acc += weight * jnp.dot(
+                        jnp.concatenate([w_k, w_k], axis=1), split[at], preferred_element_type=F32
+                    )
+                return acc
+
+            def others(s, _):
+                g = sent[1, o, s]
+                slot = jnp.where(((g >> 3) ^ a) == m3, hots[2], hots[3])
+                part3[ch, s] = target(g, slot)
+                return 0
+
+            lax.fori_loop(0, SLOTS, others, 0, unroll=SLOTS)
+            each(o, lambda k: send(2, w, k).start())
+
+            def mine(n, _):
+                out[block(n), columns(w, o)] = target(a * 8 + n, hots[0])
+                return 0
+
+            lax.fori_loop(0, 8, mine, 0, unroll=8)
+            last = choose(o, [peer(link_of(k, 3))[0] for k in range(4)])
+
+            def across(n, _):
+                part4[ch, n] = target(last * 8 + n, hots[1])
+                return 0
+
+            lax.fori_loop(0, 8, across, 0, unroll=8)
+            return 0
+
+        lax.fori_loop(0, 4, body, 0)
+
+    def fourth_exchange(w):
+        for o in range(4):
+            ch = w * 4 + o
+            send(2, w, o).wait_recv()
+            last = peer(link_of(o, 3))[0]
+
+            def came(g, o=o, ch=ch):
+                at = got[1, o, g]
+                return got3[ch][jnp.maximum(at, 0)] * jnp.where(at >= 0, 1.0, 0.0)
+
+            def across(n, _, ch=ch, last=last, came=came):
+                part4[ch, n] += came(last * 8 + n)
+                return 0
+
+            lax.fori_loop(0, 8, across, 0, unroll=2)
+            send(3, w, o).start()
+
+            def mine(n, _, o=o, came=came):
+                out[block(n), columns(w, o)] += came(a * 8 + n)
+                return 0
+
+            lax.fori_loop(0, 8, mine, 0, unroll=2)
+
+    def write(w):
+        at = pl.ds(w * 512, 512)
+        return pltpu.make_async_copy(out.at[:, at], out_hbm.at[:, at], l_sem.at[w, 3])
+
+    def finish(w):
+        def body(o, _):
+            each(o, lambda k: send(3, w, k).wait_recv())
+
+            def mine(n, _):
+                out[block(n), columns(w, o)] += got4[w * 4 + o, n]
+                return 0
+
+            lax.fori_loop(0, 8, mine, 0, unroll=2)
+            return 0
+
+        lax.fori_loop(0, 4, body, 0)
+        write(w).start()
+
+    def compute_b(h, c):
+        rows = pl.ds(h * 512 + c * 256, 256)
+        send_c(h, c).wait_recv()
+        send_f(h, c).wait_recv()
+        sources = (coef, gc, gz, gf)
+        copies = [
+            pltpu.make_async_copy(sources[q].at[blocks_b(h, c)], stage_b.at[q % 2], l_sem.at[2 + q % 2, 0])
+            for q in range(4)
+        ]
+        copies[0].start()
+        copies[1].start()
+        for q in range(4):
+            copies[q].wait()
+
+            def split_body(n, _, q=q):
+                hi, lo = pieces(stage_b[q % 2, :, :, block(n)].reshape(256, SB))
+                split_b[q * 8 + n, :, 0:SB] = hi
+                split_b[q * 8 + n, :, SB : 2 * SB] = lo
+                return 0
+
+            lax.fori_loop(0, 8, split_body, 0, unroll=2)
+            if q < 2:
+                copies[q + 2].start()
+
+        def target(reader, n, slot):
+            g = reader * 8 + n
+            acc = jnp.zeros((256, SB), F32)
+            for k in range(3):
+                src = bsrc[k, g]
+                sz, sc = src >> 4, (src >> 3) & 1
+                away = sz ^ z
+                here = (away == 0) | (away == (1 if h == 0 else 3))
+                at = jnp.where(away == 0, 0, 16) + jnp.where(sc == core, 0, 8) + (src & 7)
+                weight = jnp.where(here, integral(bpair[k, g]), 0.0)
+                w_k = hot_b[slot, n * 3 + k]
+                acc += weight * jnp.dot(
+                    split_b[at], jnp.concatenate([w_k, w_k], axis=0), preferred_element_type=F32
+                )
+            return acc
+
+        def others(n, _):
+            part_b[h, c, :, :, block(n)] = target(over_z(1 - h) * 2 + core, n, 2 - h).reshape(2, SB, SB)
+            return 0
+
+        lax.fori_loop(0, 8, others, 0, unroll=4)
+        send_b(h, c).start()
+
+        def mine(n, _):
+            out[rows, block(n)] += target(b, n, 0)
+            return 0
+
+        lax.fori_loop(0, 8, mine, 0, unroll=4)
+
+    def finish_b(h, c):
+        send_b(h, c).wait_recv()
+        cp = pltpu.make_async_copy(got_b.at[blocks_b(h, c)], stage_b.at[c], l_sem.at[2 + c, 1])
+        cp.start()
+        cp.wait()
+        out[pl.ds(h * 512 + c * 256, 256), :] += stage_b[c].reshape(256, 1024)
+
+    barrier = pltpu.get_barrier_semaphore()
+    everyone = [peer(link) for link in range(4)]
+    everyone += [(a, over_z(0) * 2 + core), (a, over_z(1) * 2 + core), partner]
+    for device in everyone:
+        pl.semaphore_signal(barrier, inc=1, device_id=device, device_id_type=MESH)
+    pl.semaphore_wait(barrier, len(everyone))
+
+    links = [
+        pltpu.make_async_copy(alinks_hbm, alinks, l_sem.at[0, 4]),
+        pltpu.make_async_copy(blinks_hbm, blinks, l_sem.at[1, 4]),
+    ]
+    for cp in links:
+        cp.start()
+    for w in range(2):
+        for o in range(4):
+            send(0, w, o).start()
+    for c in range(2):
+        for h in range(2):
+            send_z(h, c).start()
+            send_c(h, c).start()
+    for cp in links:
+        cp.wait()
+    build_alpha()
+    build_beta()
+    second_exchange(0)
+    second_exchange(1)
+    for h in range(2):
+        send_z(h, 0).wait_recv()
+        send_f(h, 0).start()
+    third_exchange(0)
+    for h in range(2):
+        send_z(h, 1).wait_recv()
+        send_f(h, 1).start()
+    third_exchange(1)
+    compute_b(0, 0)
+    compute_b(1, 0)
+    fourth_exchange(0)
+    compute_b(0, 1)
+    compute_b(1, 1)
+    fourth_exchange(1)
+    for c in range(2):
+        for h in range(2):
+            finish_b(h, c)
+    finish(0)
+    finish(1)
+    for w in range(2):
+        write(w).wait()
+        for o in range(4):
+            for i in range(4):
+                send(i, w, o).wait_send()
+    for c in range(2):
+        for h in range(2):
+            for copy in (send_z, send_c, send_f, send_b):
+                copy(h, c).wait_send()
+
+
+def named_couplings(coef, one_body, asrc, apair, alinks, bsrc, bpair, blinks, sent, got):
+    hbm = pl.BlockSpec(memory_space=pl.ANY)
+    smem = pl.BlockSpec(memory_space=pltpu.SMEM)
+    dma = pltpu.SemaphoreType.DMA
+    whole = jax.ShapeDtypeStruct((8, SB, 1024), F32)
+    return pl.pallas_call(
+        named_kernel,
+        out_shape=[
+            jax.ShapeDtypeStruct((1024, 1024), F32),
+            jax.ShapeDtypeStruct((8, 8, SB, SB), F32),
+            jax.ShapeDtypeStruct((8, SLOTS, SB, SB), F32),
+            whole,
+            whole,
+            whole,
+            whole,
+        ],
+        in_specs=[hbm, smem, smem, hbm, smem, smem, hbm, smem, smem, smem],
+        out_specs=[hbm] * 7,
+        scratch_shapes=[
+            pltpu.VMEM((1024, 1024), F32),
+            pltpu.VMEM((3, 128, SB), jnp.int32),
+            pltpu.VMEM((3, 64, SB), jnp.int32),
+            pltpu.VMEM((2, 16 + SLOTS, SB, SB), F32),
+            pltpu.VMEM((16 + SLOTS, 2 * SB, SB), BF16),
+            pltpu.VMEM((16, SB, SB), F32),
+            pltpu.VMEM((8, SLOTS, SB, SB), F32),
+            pltpu.VMEM((8, SLOTS, SB, SB), F32),
+            *[pltpu.VMEM((SLOTS, SB, SB), F32)] * 8,
+            pltpu.VMEM((8, 8, SB, SB), F32),
+            pltpu.VMEM((8, 8, SB, SB), F32),
+            pltpu.VMEM((2, 2, SB, 1024), F32),
+            pltpu.VMEM((32, 256, 2 * SB), BF16),
+            pltpu.VMEM((2, 2, 2, SB, 1024), F32),
+            pltpu.VMEM((len(HOT_SLOT), 24, SB, SB), BF16),
+            pltpu.VMEM((3, 24, SB, SB), BF16),
+            dma((4, 8)),
+            dma((4, 8)),
+            dma((4, 2, 2)),
+            dma((4, 2, 2)),
+            dma((4, 5)),
+        ],
+        compiler_params=pltpu.CompilerParams(
+            collective_id=0, has_side_effects=True, vmem_limit_bytes=61 * 2**20
+        ),
+        name="named_couplings",
+    )(
+        coef.reshape(8, SB, 1024),
+        asrc,
+        apair,
+        alinks,
+        bsrc,
+        bpair,
+        blinks,
+        one_body,
+        sent,
+        got,
+    )[0]
+
+
+def any_kernel(
     coef,
     asrc,
     apair,
@@ -431,13 +1019,13 @@
     lax.fori_loop(0, NZ, drain_z, 0)
 
 
-def couplings(coef, one_body, asrc, apair, alinks, bsrc, bpair, blinks):
+def any_couplings(coef, one_body, asrc, apair, alinks, bsrc, bpair, blinks):
     hbm = pl.BlockSpec(memory_space=pl.ANY)
     vmem = pl.BlockSpec(memory_space=pltpu.VMEM)
     smem = pl.BlockSpec(memory_space=pltpu.SMEM)
     dma = pltpu.SemaphoreType.DMA
     return pl.pallas_call(
-        kernel,
+        any_kernel,
         out_shape=[
             jax.ShapeDtypeStruct((1024, 1024), F32),
             jax.ShapeDtypeStruct((3, NCH, 1024, SB), F32),
@@ -469,9 +1057,9 @@
             dma((8,)),
         ],
         compiler_params=pltpu.CompilerParams(
-            collective_id=0, has_side_effects=True, vmem_limit_bytes=60 * 2**20
+            collective_id=1, has_side_effects=True, vmem_limit_bytes=60 * 2**20
         ),
-        name="couplings",
+        name="any_couplings",
     )(coef, asrc, apair, alinks, bsrc, bpair, blinks, one_body)[0]
 
 
@@ -487,9 +1075,8 @@
     beta_pair,
     beta_links,
 ):
-    terms = couplings(
-        coefficients,
-        one_body,
+    sent, got, most = message_tables(alpha_source, lax.axis_index("alpha"))
+    tables = (
         alpha_source.T,
         alpha_pair.T,
         alpha_links.transpose(1, 0, 2),
@@ -497,6 +1084,11 @@
         beta_pair.T,
         beta_links.transpose(1, 0, 2),
     )
+    terms = lax.cond(
+        most <= SLOTS,
+        lambda: named_couplings(coefficients, one_body, *tables, sent, got),
+        lambda: any_couplings(coefficients, one_body, *tables),
+    )
     return (alpha_energy[:, None] + beta_energy[None, :]) * coefficients + terms
 
 

time: 162 us -> 156 us (0.963)
  Pallas kernels: 155 us -> 139 us
  matrix products: 0 us -> 3.4 us
  other arithmetic: 6.02 us -> 8.99 us
  local copies, waits for them, and re-layouts: 0.01 us -> 2.47 us
    pallas_call x1, Pallas kernels: 155 us -> 139 us  [named_couplings(): pl.pallas_call(named_kernel, out_shape=[jax.ShapeDtypeStruct((1024, 1024)...]
    dot_general x0 -> x4, matrix products: none -> 3.4 us  [the longest x1 0.88 us: message_tables(): rank = jnp.einsum('trb,bc->trc', mine, before).astype(jnp.int32)]
where the time goes in v2:
time: 156 us; the launch traced here: 155 us
  Pallas kernels  139 us (89%)
  other arithmetic  8.99 us (6%)
  matrix products  3.4 us (2%)
  local copies, waits for them, and re-layouts  2.47 us (2%)
    pallas_call x1, Pallas kernels, named_couplings(): pl.pallas_call(named_kernel, out_shape=[jax.ShapeDtypeStruct((1024, 1024)...  139 us
    add x1, other arithmetic, on_device(): return (alpha_energy[:, None] + beta_energy[None, :]) * coefficients + terms  6.04 us

profile of v2, /device:TPU:0, one launch (start us, length us, event | category | flops | bytes accessed | tf_op | source)
XLA Modules:
  0.0 154.8 jit_solution(11430864849461081410)
XLA Ops:
  0.0 0.7 broadcast_shift-right-arithmetic_fusion
  0.7 0.7 broadcast_bitcast_fusion.1
  1.4 0.1 copy.23
  1.5 0.7 broadcast_bitcast_fusion
  2.2 0.1 copy.24
  2.3 0.8 fusion.6
  3.1 0.8 copy.22
  3.9 0.1 eq.20
  4.0 0.1 fusion.7
  4.1 0.8 fusion.3
  5.0 0.1 convert_reduce_fusion
  5.1 0.6 reduce_max.9
  6.4 0.8 broadcast_compare_fusion
  7.2 0.9 convolution_convert_fusion
  8.1 0.0 copy-start
  8.1 0.0 copy-start.1
  8.1 140.6 %conditional.1 = (f32[1024,1024]{1,0:T(8,128)}) conditional(s32[]{:T(128)} %convert_element_type.12, (f32[1024,1024]{1,0:T(8,128)}, s32[3,128]{1,0:T(4,128)}, s32[3,128]{1,0:T(4,128)}, s32[3,128,128]{2,1,0:T(8,128)}, s32[3,64]{1,0:T(4,128)}, /*index=5*/s32[3,64]{1,0:T(4,128)}, s32[3,64,128]{2,1,0:T(8,128)}, f32[18,18]{1,0:T(8,128)}) %tuple.39, ...), branch_computations={%region_5.6_spmd, %region_6.7_spmd.clone} | conditional | flops 67456 | bytes 156176 | solution.py:1087
  8.2 0.8 select_reduce_fusion.sent
  9.0 0.6 fusion.got
  9.6 138.9 %named_couplings.1 = (f32[1024,1024]{1,0:T(8,128)}, f32[8,8,128,128]{3,2,1,0:T(8,128)}, f32[8,13,128,128]{3,2,1,0:T(8,128)}, f32[8,128,1024]{2,1,0:T(8,128)}, f3...) custom-call(f32[8,128,1024]{2,1,0:T(8,128)} %bitcast.39, ...), custom_call_target="tpu_custom_call" | custom-call | tf_op jit(solution)/shard_map/cond/branch_1_fun/named_couplings/pallas_call | solution.py:549
  148.7 0.0 copy-done
  148.7 0.0 copy-done.1
  148.7 6.0 %multiply_add_fusion = f32[1024,1024]{1,0:T(8,128)} fusion(f32[1024,1024]{1,0:T(8,128)} %get-tuple-element.124, f32[1024,1024]{1,0:T(8,128)} %param.18, f32[1024]{0:T(1024)S(1)} %copy-done, f32[1024]{0:T(1024)S(1)} %copy-done.1), kind=kLoop, calls=%fused_computation.4 | loop fusion | flops 3145728 | bytes 12591104 | tf_op jit(solution)/shard_map/add | solution.py:1092
  (5 shorter events, 0.0 us)
Async XLA Ops:
  8.1 140.6 %copy-start = (f32[1024]{0:T(1024)S(1)}, f32[1024]{0:T(1024)}, u32[]{:S(2)}) copy-start(f32[1024]{0:T(1024)} %param.20) | copy-start | bytes 12292
  8.1 140.6 %copy-start.1 = (f32[1024]{0:T(1024)S(1)}, f32[1024]{0:T(1024)}, u32[]{:S(2)}) copy-start(f32[1024]{0:T(1024)} %param.19) | copy-start | bytes 12292

commit v3 on v2

--- a/solution.py
+++ b/solution.py
@@ -1,5 +1,3 @@
-import numpy as np
-
 import jax
 import jax.numpy as jnp
 from jax import lax
@@ -36,57 +34,73 @@
 HOT_SLOT = {m: i for i, m in enumerate(sorted({m for o in range(4) for m in reader_masks(o)}))}
 
 
-def message_masks():
-    shape = (4, 16, 16)
-    two_readers, two_sources = np.zeros(shape, np.float32), np.zeros(shape, np.float32)
-    three_sources, three_readers = np.zeros(shape, np.float32), np.zeros(shape, np.float32)
-    for o in range(4):
-        l1, l2, l3, l4 = (link_of(o, i) for i in range(4))
-        for n in range(16):
-            for v in spans((l3, l4)):
-                two_readers[o, n, n ^ LINK[l2] ^ v] = 1
-            for v in spans((l1,)):
-                two_sources[o, n, n ^ v] = 1
-            for v in spans((l1, l2)):
-                three_sources[o, n, n ^ v] = 1
-            for v in spans((l4,)):
-                three_readers[o, n, n ^ LINK[l3] ^ v] = 1
-    return two_readers, two_sources, three_sources, three_readers
-
-
-def rows_of_device():
-    pick = np.zeros((16, 2, 2, 4, 4, 16), np.float32)
-    for n in range(16):
-        for stage in range(2):
-            for o in range(4):
-                pick[n, stage, 0, o, o, n] = 1
-                pick[n, stage, 1, o, o, n ^ LINK[link_of(o, stage + 1)]] = 1
-    return pick.reshape(16, 2, 8, 64)
-
-
-def message_tables(source, me):
-    two_readers, two_sources, three_sources, three_readers = (
-        jnp.asarray(m.reshape(64, 16)) for m in message_masks()
-    )
-    blocks = jnp.arange(128, dtype=jnp.int32)
-    by_reader = source.reshape(16, 24)
-    named = jnp.any(by_reader[:, :, None] == blocks, axis=1).astype(F32)
-    devices = jnp.arange(16, dtype=jnp.int32)
-    fed = jnp.any((source >> 3)[:, :, None] == devices, axis=1).astype(F32)
-    two = (jnp.dot(two_readers, named) > 0.5) & (jnp.repeat(two_sources, 8, axis=1) > 0.5)
-    three = (jnp.dot(three_sources, fed.T) > 0.5) & (jnp.repeat(three_readers, 8, axis=1) > 0.5)
-    masks = jnp.stack([two, three]).astype(F32)
-    most = jnp.max(jnp.sum(masks, axis=2))
-    pick = lax.dynamic_index_in_dim(jnp.asarray(rows_of_device()), me, 0, keepdims=False)
-    mine = jnp.einsum("trm,tmb->trb", pick, masks)
-    before = jnp.asarray(np.triu(np.ones((128, 128), np.float32), 1))
-    rank = jnp.einsum("trb,bc->trc", mine, before).astype(jnp.int32)
-    here = mine > 0.5
-    slots = jnp.arange(16, dtype=jnp.int32)
-    chosen = here[:, :4, None, :] & (rank[:, :4, None, :] == slots[:, None])
-    sent = jnp.sum(jnp.where(chosen, blocks, 0), axis=3)
-    got = jnp.where(here[:, 4:], jnp.minimum(rank[:, 4:], SLOTS - 1), -1)
-    return sent, got, most
+def table_kernel(source, slots, fits):
+    me = lax.axis_index("alpha")
+
+    def iota(shape, axis):
+        return lax.broadcasted_iota(jnp.int32, shape, axis)
+
+    def mask_of(order, i):
+        link = (order + i) % 4
+        return jnp.where(link == 0, 1, jnp.where(link == 1, 3, jnp.where(link == 2, 4, 12)))
+
+    def ones(mask):
+        return jnp.where(mask, 1.0, 0.0).astype(BF16)
+
+    def dot(left, right, axis=0):
+        return lax.dot_general(left, right, (((1,), (axis,)), ((), ())), preferred_element_type=F32)
+
+    row, lane = iota((64, 128), 0), iota((64, 128), 1)
+    order, sender = row // 16, row % 16
+    m1, m2, m3, m4 = (mask_of(order, i) for i in range(4))
+    apart = (lane >> 3) ^ sender
+    reader = apart ^ m2
+    two_readers = (reader == 0) | (reader == m3) | (reader == m4) | (reader == (m3 ^ m4))
+    two_sources = (apart == 0) | (apart == m1)
+    device = lane ^ sender
+    three_sources = (device == 0) | (device == m1) | (device == m2) | (device == (m1 ^ m2))
+    three_readers = (apart == m3) | (apart == (m3 ^ m4))
+    which = iota((128, 128), 0)
+    named, fed = which < 0, which < 0
+    for k in range(3):
+        line = source[k : k + 1, :]
+        named = named | (line == which)
+        fed = fed | ((line >> 3) == which)
+    two = two_sources & (dot(ones(two_readers), ones(named), 1) > 0.5)
+    three = three_readers & (dot(ones(three_sources), ones(fed)) > 0.5)
+    before = ones(which < iota((128, 128), 1))
+    row, lane = iota((8, 64), 0), iota((8, 64), 1)
+    order = row % 4
+    at = iota((8, 128), 1)
+    most = jnp.int32(0)
+    for stage, messages in enumerate((two, three)):
+        node = jnp.where(row < 4, me, me ^ mask_of(order, stage + 1))
+        mine = dot(ones(lane == order * 16 + node), ones(messages))
+        rank = dot(mine.astype(BF16), before).astype(jnp.int32)
+        here = mine > 0.5
+        chosen = jnp.zeros((8, 128), jnp.int32)
+        for s in range(SLOTS):
+            block = jnp.sum(jnp.where(here & (rank == s), at, 0), axis=1, keepdims=True)
+            chosen = jnp.where(at == s, block, chosen)
+        got = jnp.where(here, jnp.minimum(rank, SLOTS - 1), -1)
+        slots[stage] = jnp.where(iota((8, 128), 0) < 4, chosen, got)
+        count = jnp.sum(jnp.where(messages, 1, 0), axis=1, keepdims=True)
+        most = jnp.maximum(most, jnp.max(count))
+    fits[0, 0] = jnp.where(most <= SLOTS, 1, 0)
+
+
+def message_tables(source):
+    vmem = pl.BlockSpec(memory_space=pltpu.VMEM)
+    return pl.pallas_call(
+        table_kernel,
+        out_shape=[
+            jax.ShapeDtypeStruct((2, 8, 128), jnp.int32),
+            jax.ShapeDtypeStruct((1, 1), jnp.int32),
+        ],
+        in_specs=[vmem],
+        out_specs=[vmem, pl.BlockSpec(memory_space=pltpu.SMEM)],
+        name="message_tables",
+    )(source)
 
 
 def named_kernel(
@@ -98,8 +112,9 @@
     bpair,
     blinks_hbm,
     table,
-    sent,
-    got,
+    slots,
+    energy_a,
+    energy_b,
     out_hbm,
     got1,
     got2,
@@ -118,7 +133,8 @@
     *rest,
 ):
     got3, rest = rest[:8], rest[8:]
-    part4, got4, stage_b, split_b, part_b, hot, hot_b, s_sem, r_sem, zs_sem, zr_sem, l_sem = rest
+    part4, got4, stage_b, split_b, part_b, hot, hot_b, rows_a, *rest = rest
+    at_own, weight_own, at_sent, weight_sent, hot_sent, s_sem, r_sem, zs_sem, zr_sem, l_sem = rest
     a = lax.axis_index("alpha")
     b = lax.axis_index("beta")
     y, x, z, core = a // 4, a % 4, b // 2, b % 2
@@ -245,10 +261,56 @@
             def body(n, _, slot=slot, reader=reader):
                 for k in range(3):
                     row = alinks[k, pl.ds(reader * 8 + n, 1), :]
-                    hot[slot, n * 3 + k] = signed_hot(row).T.astype(BF16)
+                    hot[slot, k * 8 + n] = signed_hot(row).T.astype(BF16)
                 return 0
 
             lax.fori_loop(0, 8, body, 0, unroll=4)
+
+    def plan():
+        def body(o, _):
+            m1 = choose(o, [LINK[link_of(k, 0)] for k in range(4)])
+            m2 = choose(o, [LINK[link_of(k, 1)] for k in range(4)])
+            m3 = choose(o, [LINK[link_of(k, 2)] for k in range(4)])
+            last = choose(o, [peer(link_of(k, 3))[0] for k in range(4)])
+            hots = [
+                choose(o, [HOT_SLOT[reader_masks(k)[role]] for k in range(4)])
+                for role in range(2, 4)
+            ]
+
+            def entry(g, k):
+                src = asrc[k, g]
+                apart = (src >> 3) ^ a
+                inner = src & 7
+                over_two = (apart == m2) | (apart == (m1 ^ m2))
+                here = over_two | (apart == 0) | (apart == m1)
+                arrived = 16 + jnp.maximum(slots[0, 4 + o, src], 0)
+                at = jnp.where(over_two, arrived, jnp.where(apart == m1, 8 + inner, inner))
+                return at, jnp.where(here, integral(apair[k, g]), 0.0)
+
+            def own_entries(n, _):
+                for role, reader in enumerate((a, last)):
+                    for k in range(3):
+                        at, weight = entry(reader * 8 + n, k)
+                        at_own[o, role * 24 + n * 3 + k] = at
+                        weight_own[o, role * 24 + n * 3 + k] = weight
+                return 0
+
+            lax.fori_loop(0, 8, own_entries, 0)
+
+            def sent_entries(s, _):
+                g = slots[1, o, s]
+                hot_sent[o, s] = jnp.where(((g >> 3) ^ a) == m3, hots[0], hots[1])
+                hot_sent[o, SLOTS + s] = g & 7
+                for k in range(3):
+                    at, weight = entry(g, k)
+                    at_sent[o, s * 3 + k] = at
+                    weight_sent[o, s * 3 + k] = weight
+                return 0
+
+            lax.fori_loop(0, SLOTS, sent_entries, 0)
+            return 0
+
+        lax.fori_loop(0, 4, body, 0)
 
     def build_beta():
         for slot in range(3):
@@ -311,7 +373,7 @@
             lax.fori_loop(0, 16, hold, 0, unroll=4)
 
             def fill(s, _):
-                wanted = sent[0, o, s]
+                wanted = slots[0, o, s]
                 at = jnp.where((wanted >> 3) == a, 0, 8) + (wanted & 7)
                 pack[w * 4 + o, s] = held[at]
                 return 0
@@ -327,11 +389,8 @@
             ready(w, o, 1)
             buf = o % 2
             ch = w * 4 + o
-            m1 = choose(o, [LINK[link_of(k, 0)] for k in range(4)])
-            m2 = choose(o, [LINK[link_of(k, 1)] for k in range(4)])
-            m3 = choose(o, [LINK[link_of(k, 2)] for k in range(4)])
             hots = [
-                choose(o, [HOT_SLOT[reader_masks(k)[role]] for k in range(4)]) for role in range(4)
+                choose(o, [HOT_SLOT[reader_masks(k)[role]] for k in range(4)]) for role in range(2)
             ]
 
             def split_body(n, _):
@@ -342,41 +401,38 @@
 
             lax.fori_loop(0, 16 + SLOTS, split_body, 0, unroll=8)
 
-            def target(g, slot):
+            def product(at, w_k):
+                return jnp.dot(
+                    jnp.concatenate([w_k, w_k], axis=1), split[at], preferred_element_type=F32
+                )
+
+            def others(s, _):
                 acc = jnp.zeros((SB, SB), F32)
                 for k in range(3):
-                    src = asrc[k, g]
-                    apart = (src >> 3) ^ a
-                    inner = src & 7
-                    over_two = (apart == m2) | (apart == (m1 ^ m2))
-                    here = over_two | (apart == 0) | (apart == m1)
-                    arrived = 16 + jnp.maximum(got[0, o, src], 0)
-                    at = jnp.where(over_two, arrived, jnp.where(apart == m1, 8 + inner, inner))
-                    weight = jnp.where(here, integral(apair[k, g]), 0.0)
-                    w_k = hot[slot, (g & 7) * 3 + k]
-                    acc += weight * jnp.dot(
-                        jnp.concatenate([w_k, w_k], axis=1), split[at], preferred_element_type=F32
-                    )
-                return acc
-
-            def others(s, _):
-                g = sent[1, o, s]
-                slot = jnp.where(((g >> 3) ^ a) == m3, hots[2], hots[3])
-                part3[ch, s] = target(g, slot)
+                    w_k = hot[hot_sent[o, s], k * 8 + hot_sent[o, SLOTS + s]]
+                    acc += weight_sent[o, s * 3 + k] * product(at_sent[o, s * 3 + k], w_k)
+                part3[ch, s] = acc
                 return 0
 
             lax.fori_loop(0, SLOTS, others, 0, unroll=SLOTS)
             each(o, lambda k: send(2, w, k).start())
 
+            def target(role, n):
+                acc = jnp.zeros((SB, SB), F32)
+                for k in range(3):
+                    e = role * 24 + n * 3 + k
+                    acc += weight_own[o, e] * product(at_own[o, e], hot[hots[role], k * 8 + n])
+                return acc
+
             def mine(n, _):
-                out[block(n), columns(w, o)] = target(a * 8 + n, hots[0])
+                energy = rows_a[n] + energy_b[:, columns(w, o)]
+                out[block(n), columns(w, o)] += energy * stage[buf, n] + target(0, n)
                 return 0
 
             lax.fori_loop(0, 8, mine, 0, unroll=8)
-            last = choose(o, [peer(link_of(k, 3))[0] for k in range(4)])
 
             def across(n, _):
-                part4[ch, n] = target(last * 8 + n, hots[1])
+                part4[ch, n] = target(1, n)
                 return 0
 
             lax.fori_loop(0, 8, across, 0, unroll=8)
@@ -391,7 +447,7 @@
             last = peer(link_of(o, 3))[0]
 
             def came(g, o=o, ch=ch):
-                at = got[1, o, g]
+                at = slots[1, 4 + o, g]
                 return got3[ch][jnp.maximum(at, 0)] * jnp.where(at >= 0, 1.0, 0.0)
 
             def across(n, _, ch=ch, last=last, came=came):
@@ -508,26 +564,31 @@
     for cp in links:
         cp.wait()
     build_alpha()
+    for n in range(8):
+        rows_a[n] = jnp.broadcast_to(energy_a[n : n + 1, :], (SB, SB)).T
+    out[...] = jnp.zeros_like(out)
+    plan()
+    second_exchange(0)
     build_beta()
-    second_exchange(0)
     second_exchange(1)
     for h in range(2):
         send_z(h, 0).wait_recv()
         send_f(h, 0).start()
+    for h in range(2):
+        compute_b(h, 0)
     third_exchange(0)
     for h in range(2):
         send_z(h, 1).wait_recv()
         send_f(h, 1).start()
     third_exchange(1)
-    compute_b(0, 0)
-    compute_b(1, 0)
+    for h in range(2):
+        compute_b(h, 1)
     fourth_exchange(0)
-    compute_b(0, 1)
-    compute_b(1, 1)
+    for h in range(2):
+        finish_b(h, 0)
     fourth_exchange(1)
-    for c in range(2):
-        for h in range(2):
-            finish_b(h, c)
+    for h in range(2):
+        finish_b(h, 1)
     finish(0)
     finish(1)
     for w in range(2):
@@ -541,9 +602,10 @@
                 copy(h, c).wait_send()
 
 
-def named_couplings(coef, one_body, asrc, apair, alinks, bsrc, bpair, blinks, sent, got):
+def named_sigma(coef, energy_a, energy_b, one_body, asrc, apair, alinks, bsrc, bpair, blinks, slots):
     hbm = pl.BlockSpec(memory_space=pl.ANY)
     smem = pl.BlockSpec(memory_space=pltpu.SMEM)
+    vmem = pl.BlockSpec(memory_space=pltpu.VMEM)
     dma = pltpu.SemaphoreType.DMA
     whole = jax.ShapeDtypeStruct((8, SB, 1024), F32)
     return pl.pallas_call(
@@ -557,7 +619,7 @@
             whole,
             whole,
         ],
-        in_specs=[hbm, smem, smem, hbm, smem, smem, hbm, smem, smem, smem],
+        in_specs=[hbm, smem, smem, hbm, smem, smem, hbm, smem, smem, vmem, vmem],
         out_specs=[hbm] * 7,
         scratch_shapes=[
             pltpu.VMEM((1024, 1024), F32),
@@ -576,6 +638,12 @@
             pltpu.VMEM((2, 2, 2, SB, 1024), F32),
             pltpu.VMEM((len(HOT_SLOT), 24, SB, SB), BF16),
             pltpu.VMEM((3, 24, SB, SB), BF16),
+            pltpu.VMEM((8, SB, SB), F32),
+            pltpu.SMEM((4, 48), jnp.int32),
+            pltpu.SMEM((4, 48), F32),
+            pltpu.SMEM((4, 3 * SLOTS), jnp.int32),
+            pltpu.SMEM((4, 3 * SLOTS), F32),
+            pltpu.SMEM((4, 2 * SLOTS), jnp.int32),
             dma((4, 8)),
             dma((4, 8)),
             dma((4, 2, 2)),
@@ -585,7 +653,7 @@
         compiler_params=pltpu.CompilerParams(
             collective_id=0, has_side_effects=True, vmem_limit_bytes=61 * 2**20
         ),
-        name="named_couplings",
+        name="named_sigma",
     )(
         coef.reshape(8, SB, 1024),
         asrc,
@@ -595,8 +663,9 @@
         bpair,
         blinks,
         one_body,
-        sent,
-        got,
+        slots,
+        energy_a.reshape(8, SB),
+        energy_b.reshape(1, 1024),
     )[0]
 
 
@@ -1075,7 +1144,6 @@
     beta_pair,
     beta_links,
 ):
-    sent, got, most = message_tables(alpha_source, lax.axis_index("alpha"))
     tables = (
         alpha_source.T,
         alpha_pair.T,
@@ -1084,12 +1152,16 @@
         beta_pair.T,
         beta_links.transpose(1, 0, 2),
     )
-    terms = lax.cond(
-        most <= SLOTS,
-        lambda: named_couplings(coefficients, one_body, *tables, sent, got),
-        lambda: any_couplings(coefficients, one_body, *tables),
-    )
-    return (alpha_energy[:, None] + beta_energy[None, :]) * coefficients + terms
+    slots, fits = message_tables(tables[0])
+
+    def with_slots():
+        return named_sigma(coefficients, alpha_energy, beta_energy, one_body, *tables, slots)
+
+    def without_slots():
+        terms = any_couplings(coefficients, one_body, *tables)
+        return (alpha_energy[:, None] + beta_energy[None, :]) * coefficients + terms
+
+    return lax.cond(fits[0, 0] == 1, with_slots, without_slots)
 
 
 def solution(mesh):

time: 156 us -> 138 us (0.88)
  other arithmetic: 8.99 us -> 0 us
  Pallas kernels: 139 us -> 131 us
  matrix products: 3.4 us -> 0 us
  local copies, waits for them, and re-layouts: 2.47 us -> 4.79 us
    pallas_call x1 -> x2, Pallas kernels: 139 us -> 131 us  [the longest x1 130 us: named_sigma(): pl.pallas_call(named_kernel, out_shape=[jax.ShapeDtypeStruct((1024, 1024)...]
    add x1 -> x0, other arithmetic: 6.04 us -> none  [on_device(): return (alpha_energy[:, None] + beta_energy[None, :]) * coefficients + terms]
    unnamed x5 -> x1, local copies, waits for them, and re-layouts: 0.8 us -> 4.79 us
    dot_general x4 -> x0, matrix products: 3.4 us -> none  [the longest x1 0.88 us: message_tables(): rank = jnp.einsum('trb,bc->trc', mine, before).astype(jnp.int32)]
    gt x4 -> x0, local copies, waits for them, and re-layouts: 1.56 us -> none  [the longest x2 0.78 us: message_tables(): jnp.repeat(three_readers, 8, axis=1) > 0.5]
where the time goes in v3:
time: 138 us; the launch traced here: 137 us
  Pallas kernels  131 us (95%)
  local copies, waits for them, and re-layouts  4.79 us (3%)
    pallas_call x1, Pallas kernels, named_sigma(): pl.pallas_call(named_kernel, out_shape=[jax.ShapeDtypeStruct((1024, 1024)...  130 us
    unnamed x1, local copies, waits for them, and re-layouts  4.79 us

profile of v3, /device:TPU:0, one launch (start us, length us, event | category | flops | bytes accessed | tf_op | source)
XLA Modules:
  0.0 137.1 jit_solution(6560747985504817685)
XLA Ops:
  0.0 1.5 %message_tables.1 = (s32[2,8,128]{2,1,0:T(8,128)S(1)}, s32[1,1]{1,0:T(1,128)}) custom-call(s32[3,128]{1,0:T(4,128)} %bitcast.15), custom_call_target="tpu_custom_call" | custom-call | tf_op jit(solution)/shard_map/message_tables/pallas_call | solution.py:94
  2.2 130.1 %conditional.1 = (f32[1024,1024]{1,0:T(8,128)}) conditional(s32[]{:T(128)} %bitcast.4, (f32[1024]{0:T(1024)}, f32[1024]{0:T(1024)}, f32[1024,1024]{1,0:T(8,128)}, s32[3,128]{1,0:T(4,128)}, s32[3,128]{1,0:T(4,128)}, /*index=5*/s32[3,128,128]{2,1,0:T(8,128)}, s32[3,64]{1,0:T(4,128)}, s32[3,64]{1,0:T(4,128)}, s32[3,64,128]{2,1,0:T(8,128)}, ...), branch_computations={%region_0.0_spmd, %region_1.0_spmd} | conditional | flops 3145728 | bytes 12623936 | solution.py:1164
  2.2 129.9 %named_sigma.1 = (f32[1024,1024]{1,0:T(8,128)}, f32[8,8,128,128]{3,2,1,0:T(8,128)}, f32[8,13,128,128]{3,2,1,0:T(8,128)}, f32[8,128,1024]{2,1,0:T(8,128)}, f32[8,...) custom-call(f32[8,128,1024]{2,1,0:T(8,128)} %bitcast.10, s32[3,128]{1,0:T(4,128)} %get-tuple-element.62.asrc, ...), custom_call_target="tpu_custom_call" | custom-call | tf_op jit(solution)/shard_map/cond/branch_1_fun/named_sigma/pallas_call | solution.py:611
  132.4 4.8 %copy.16 = f32[1024,1024]{1,0:T(8,128)} copy(f32[1024,1024]{1,0:T(8,128)} %get-tuple-element.77) | data formatting | bytes 8388608

commit v4 on v3

--- a/solution.py
+++ b/solution.py
@@ -116,6 +116,7 @@
     energy_a,
     energy_b,
     out_hbm,
+    tail,
     got1,
     got2,
     gz,
@@ -181,7 +182,12 @@
     def send(i, w, o):
         ch = w * 4 + o
         src = (coef.at[:, :, columns(w, o)], pack.at[ch], part3.at[ch], part4.at[ch])[i]
-        dst = got3[ch] if i == 2 else (got1, got2, None, got4)[i].at[ch]
+        if i == 2:
+            dst = got3[ch]
+        elif i == 3:
+            dst = (got4, tail)[w].at[o]
+        else:
+            dst = (got1, got2)[i].at[ch]
         return pltpu.make_async_remote_copy(
             src_ref=src,
             dst_ref=dst,
@@ -226,7 +232,7 @@
 
     def send_b(h, c):
         return pltpu.make_async_remote_copy(
-            src_ref=part_b.at[h, c],
+            src_ref=part_b.at[h],
             dst_ref=got_b.at[blocks_b(h, c)],
             send_sem=zs_sem.at[3, h, c],
             recv_sem=zr_sem.at[3, h, c],
@@ -467,19 +473,15 @@
         at = pl.ds(w * 512, 512)
         return pltpu.make_async_copy(out.at[:, at], out_hbm.at[:, at], l_sem.at[w, 3])
 
-    def finish(w):
-        def body(o, _):
-            each(o, lambda k: send(3, w, k).wait_recv())
-
-            def mine(n, _):
-                out[block(n), columns(w, o)] += got4[w * 4 + o, n]
+    def finish():
+        for o in range(4):
+            send(3, 0, o).wait_recv()
+
+            def mine(n, _, o=o):
+                out[block(n), columns(0, o)] += got4[o, n]
                 return 0
 
             lax.fori_loop(0, 8, mine, 0, unroll=2)
-            return 0
-
-        lax.fori_loop(0, 4, body, 0)
-        write(w).start()
 
     def compute_b(h, c):
         rows = pl.ds(h * 512 + c * 256, 256)
@@ -522,9 +524,11 @@
             return acc
 
         def others(n, _):
-            part_b[h, c, :, :, block(n)] = target(over_z(1 - h) * 2 + core, n, 2 - h).reshape(2, SB, SB)
-            return 0
-
+            part_b[h, :, :, block(n)] = target(over_z(1 - h) * 2 + core, n, 2 - h).reshape(2, SB, SB)
+            return 0
+
+        if c == 1:
+            send_b(h, 0).wait_send()
         lax.fori_loop(0, 8, others, 0, unroll=4)
         send_b(h, c).start()
 
@@ -589,8 +593,11 @@
     fourth_exchange(1)
     for h in range(2):
         finish_b(h, 1)
-    finish(0)
-    finish(1)
+    write(1).start()
+    finish()
+    write(0).start()
+    for o in range(4):
+        send(3, 1, o).wait_recv()
     for w in range(2):
         write(w).wait()
         for o in range(4):
@@ -598,8 +605,10 @@
                 send(i, w, o).wait_send()
     for c in range(2):
         for h in range(2):
-            for copy in (send_z, send_c, send_f, send_b):
+            for copy in (send_z, send_c, send_f):
                 copy(h, c).wait_send()
+            if c == 1:
+                send_b(h, c).wait_send()
 
 
 def named_sigma(coef, energy_a, energy_b, one_body, asrc, apair, alinks, bsrc, bpair, blinks, slots):
@@ -612,6 +621,7 @@
         named_kernel,
         out_shape=[
             jax.ShapeDtypeStruct((1024, 1024), F32),
+            jax.ShapeDtypeStruct((4, 8, SB, SB), F32),
             jax.ShapeDtypeStruct((8, 8, SB, SB), F32),
             jax.ShapeDtypeStruct((8, SLOTS, SB, SB), F32),
             whole,
@@ -620,7 +630,7 @@
             whole,
         ],
         in_specs=[hbm, smem, smem, hbm, smem, smem, hbm, smem, smem, vmem, vmem],
-        out_specs=[hbm] * 7,
+        out_specs=[hbm] * 8,
         scratch_shapes=[
             pltpu.VMEM((1024, 1024), F32),
             pltpu.VMEM((3, 128, SB), jnp.int32),
@@ -632,10 +642,10 @@
             pltpu.VMEM((8, SLOTS, SB, SB), F32),
             *[pltpu.VMEM((SLOTS, SB, SB), F32)] * 8,
             pltpu.VMEM((8, 8, SB, SB), F32),
-            pltpu.VMEM((8, 8, SB, SB), F32),
+            pltpu.VMEM((4, 8, SB, SB), F32),
             pltpu.VMEM((2, 2, SB, 1024), F32),
             pltpu.VMEM((32, 256, 2 * SB), BF16),
-            pltpu.VMEM((2, 2, 2, SB, 1024), F32),
+            pltpu.VMEM((2, 2, SB, 1024), F32),
             pltpu.VMEM((len(HOT_SLOT), 24, SB, SB), BF16),
             pltpu.VMEM((3, 24, SB, SB), BF16),
             pltpu.VMEM((8, SB, SB), F32),
@@ -651,7 +661,7 @@
             dma((4, 5)),
         ],
         compiler_params=pltpu.CompilerParams(
-            collective_id=0, has_side_effects=True, vmem_limit_bytes=61 * 2**20
+            collective_id=0, has_side_effects=True, vmem_limit_bytes=109 * 2**19
         ),
         name="named_sigma",
     )(
@@ -666,7 +676,35 @@
         slots,
         energy_a.reshape(8, SB),
         energy_b.reshape(1, 1024),
-    )[0]
+    )[:2]
+
+
+def finish_kernel(part, tail, sigma, half, sems):
+    first = pl.ds(0, 512)
+    copies = [pltpu.make_async_copy(part.at[:, first], sigma.at[:, first], sems.at[4])]
+    copies[0].start()
+    for o in range(4):
+        at = pl.ds(512 + o * SB, SB)
+        for n in range(8):
+            rows = pl.ds(n * SB, SB)
+            half[o, rows, :] = part[rows, at] + tail[o, n]
+        copies.append(pltpu.make_async_copy(half.at[o], sigma.at[:, at], sems.at[o]))
+        copies[-1].start()
+    for copy in copies:
+        copy.wait()
+
+
+def finish_sigma(part, tail):
+    vmem = pl.BlockSpec(memory_space=pltpu.VMEM)
+    return pl.pallas_call(
+        finish_kernel,
+        out_shape=jax.ShapeDtypeStruct((1024, 1024), F32),
+        in_specs=[vmem, vmem],
+        out_specs=pl.BlockSpec(memory_space=pl.ANY),
+        scratch_shapes=[pltpu.VMEM((4, 1024, SB), F32), pltpu.SemaphoreType.DMA((5,))],
+        compiler_params=pltpu.CompilerParams(vmem_limit_bytes=16 * 2**20),
+        name="finish_sigma",
+    )(part, tail)
 
 
 def any_kernel(
@@ -1126,7 +1164,7 @@
             dma((8,)),
         ],
         compiler_params=pltpu.CompilerParams(
-            collective_id=1, has_side_effects=True, vmem_limit_bytes=60 * 2**20
+            collective_id=1, has_side_effects=True, vmem_limit_bytes=109 * 2**19
         ),
         name="any_couplings",
     )(coef, asrc, apair, alinks, bsrc, bpair, blinks, one_body)[0]
@@ -1159,9 +1197,10 @@
 
     def without_slots():
         terms = any_couplings(coefficients, one_body, *tables)
-        return (alpha_energy[:, None] + beta_energy[None, :]) * coefficients + terms
-
-    return lax.cond(fits[0, 0] == 1, with_slots, without_slots)
+        diagonal = (alpha_energy[:, None] + beta_energy[None, :]) * coefficients
+        return diagonal + terms, jnp.zeros((4, 8, SB, SB), F32)
+
+    return finish_sigma(*lax.cond(fits[0, 0] == 1, lambda: tuple(with_slots()), without_slots))
 
 
 def solution(mesh):

time: 138 us -> 133 us (0.964)
  local copies, waits for them, and re-layouts: 4.79 us -> 0 us
    unnamed x1 -> x0, local copies, waits for them, and re-layouts: 4.79 us -> none
    pallas_call x0 -> x1, Pallas kernels: none -> 2.05 us  [finish_sigma(): pl.pallas_call(finish_kernel, out_shape=jax.ShapeDtypeStruct((1024, 1024)...]
    pallas_call x1, Pallas kernels: 130 us -> 128 us  [named_sigma(): pl.pallas_call(named_kernel, out_shape=[jax.ShapeDtypeStruct((1024, 1024)...]
where the time goes in v4:
time: 133 us
  Pallas kernels  132 us (99%)
    pallas_call x1, Pallas kernels, named_sigma(): pl.pallas_call(named_kernel, out_shape=[jax.ShapeDtypeStruct((1024, 1024)...  128 us

profile of v4, /device:TPU:0, one launch (start us, length us, event | category | flops | bytes accessed | tf_op | source)
XLA Modules:
  0.0 132.7 jit_solution(12044142298166805235)
XLA Ops:
  0.0 1.5 %message_tables.1 = (s32[2,8,128]{2,1,0:T(8,128)S(1)}, s32[1,1]{1,0:T(1,128)}) custom-call(s32[3,128]{1,0:T(4,128)} %bitcast.15), custom_call_target="tpu_custom_call" | custom-call | tf_op jit(solution)/shard_map/message_tables/pallas_call | solution.py:94
  2.2 128.2 %conditional.1 = (f32[1024,1024]{1,0:T(8,128)S(1)}, f32[4,8,128,128]{3,2,1,0:T(8,128)S(1)}) conditional(s32[]{:T(128)} %bitcast.4, (f32[1024]{0:T(1024)}, f32[1024]{0:T(1024)}, f32[1024,1024]{1,0:T(8,128)}, s32[3,128]{1,0:T(4,128)}, s32[3,128]{1,0:T(4,128)}, /*index=5*/s32[3,128,128]{2,1,0:T(8,128)}, s32[3,64]{1,0:T(4,128)}, s32[3,64]{1,0:T(4,128)}, ...), branch_computations={%region_0.0_spmd, %region_1.0_spmd} | conditional | flops 3145728 | bytes 31498344 | solution.py:1203
  2.2 128.0 %named_sigma.1 = (f32[1024,1024]{1,0:T(8,128)S(1)}, f32[4,8,128,128]{3,2,1,0:T(8,128)S(1)}, f32[8,8,128,128]{3,2,1,0:T(8,128)}, f32[8,13,128,128]{3,2,1,0:T(8,12...) custom-call(f32[8,128,1024]{2,1,0:T(8,128)} %bitcast.10, ...), custom_call_target="tpu_custom_call" | custom-call | tf_op jit(solution)/shard_map/cond/branch_1_fun/named_sigma/pallas_call | solution.py:620
  130.5 2.0 %finish_sigma.1 = f32[1024,1024]{1,0:T(8,128)} custom-call(f32[1024,1024]{1,0:T(8,128)S(1)} %get-tuple-element.77.part, f32[4,8,128,128]{3,2,1,0:T(8,128)S(1)} %get-tuple-element.78.tail), custom_call_target="tpu_custom_call" | custom-call | tf_op jit(solution)/shard_map/finish_sigma/pallas_call | solution.py:699

commit v5 on v4

--- a/solution.py
+++ b/solution.py
@@ -1,3 +1,5 @@
+import functools
+
 import jax
 import jax.numpy as jnp
 from jax import lax
@@ -10,7 +12,7 @@
 SB = 128
 NCH = 4
 NZ = 8
-SLOTS = 13
+ROOMS = (12, 13)
 
 LINK = (1, 3, 4, 12)
 
@@ -34,7 +36,7 @@
 HOT_SLOT = {m: i for i, m in enumerate(sorted({m for o in range(4) for m in reader_masks(o)}))}
 
 
-def table_kernel(source, slots, fits):
+def table_kernel(source, slots, choice):
     me = lax.axis_index("alpha")
 
     def iota(shape, axis):
@@ -79,14 +81,14 @@
         rank = dot(mine.astype(BF16), before).astype(jnp.int32)
         here = mine > 0.5
         chosen = jnp.zeros((8, 128), jnp.int32)
-        for s in range(SLOTS):
+        for s in range(ROOMS[-1]):
             block = jnp.sum(jnp.where(here & (rank == s), at, 0), axis=1, keepdims=True)
             chosen = jnp.where(at == s, block, chosen)
-        got = jnp.where(here, jnp.minimum(rank, SLOTS - 1), -1)
+        got = jnp.where(here, jnp.minimum(rank, ROOMS[-1] - 1), -1)
         slots[stage] = jnp.where(iota((8, 128), 0) < 4, chosen, got)
         count = jnp.sum(jnp.where(messages, 1, 0), axis=1, keepdims=True)
         most = jnp.maximum(most, jnp.max(count))
-    fits[0, 0] = jnp.where(most <= SLOTS, 1, 0)
+    choice[0, 0] = sum(jnp.where(most > room, 1, 0) for room in ROOMS)
 
 
 def message_tables(source):
@@ -104,6 +106,7 @@
 
 
 def named_kernel(
+    room,
     coef,
     asrc,
     apair,
@@ -306,14 +309,14 @@
             def sent_entries(s, _):
                 g = slots[1, o, s]
                 hot_sent[o, s] = jnp.where(((g >> 3) ^ a) == m3, hots[0], hots[1])
-                hot_sent[o, SLOTS + s] = g & 7
+                hot_sent[o, room + s] = g & 7
                 for k in range(3):
                     at, weight = entry(g, k)
                     at_sent[o, s * 3 + k] = at
                     weight_sent[o, s * 3 + k] = weight
                 return 0
 
-            lax.fori_loop(0, SLOTS, sent_entries, 0)
+            lax.fori_loop(0, room, sent_entries, 0)
             return 0
 
         lax.fori_loop(0, 4, body, 0)
@@ -342,7 +345,7 @@
         if second:
             copies.append(
                 pltpu.make_async_copy(
-                    got2.at[w * 4 + o], stage.at[buf, pl.ds(16, SLOTS)], l_sem.at[buf, 2]
+                    got2.at[w * 4 + o], stage.at[buf, pl.ds(16, room)], l_sem.at[buf, 2]
                 )
             )
         return copies
@@ -384,7 +387,7 @@
                 pack[w * 4 + o, s] = held[at]
                 return 0
 
-            lax.fori_loop(0, SLOTS, fill, 0)
+            lax.fori_loop(0, room, fill, 0)
             each(o, lambda k: send(1, w, k).start())
             return 0
 
@@ -405,7 +408,7 @@
                 split[n, SB : 2 * SB, :] = lo
                 return 0
 
-            lax.fori_loop(0, 16 + SLOTS, split_body, 0, unroll=8)
+            lax.fori_loop(0, 16 + room, split_body, 0, unroll=8)
 
             def product(at, w_k):
                 return jnp.dot(
@@ -415,12 +418,12 @@
             def others(s, _):
                 acc = jnp.zeros((SB, SB), F32)
                 for k in range(3):
-                    w_k = hot[hot_sent[o, s], k * 8 + hot_sent[o, SLOTS + s]]
+                    w_k = hot[hot_sent[o, s], k * 8 + hot_sent[o, room + s]]
                     acc += weight_sent[o, s * 3 + k] * product(at_sent[o, s * 3 + k], w_k)
                 part3[ch, s] = acc
                 return 0
 
-            lax.fori_loop(0, SLOTS, others, 0, unroll=SLOTS)
+            lax.fori_loop(0, room, others, 0, unroll=room)
             each(o, lambda k: send(2, w, k).start())
 
             def target(role, n):
@@ -611,19 +614,21 @@
                 send_b(h, c).wait_send()
 
 
-def named_sigma(coef, energy_a, energy_b, one_body, asrc, apair, alinks, bsrc, bpair, blinks, slots):
+def named_sigma(
+    room, coef, energy_a, energy_b, one_body, asrc, apair, alinks, bsrc, bpair, blinks, slots
+):
     hbm = pl.BlockSpec(memory_space=pl.ANY)
     smem = pl.BlockSpec(memory_space=pltpu.SMEM)
     vmem = pl.BlockSpec(memory_space=pltpu.VMEM)
     dma = pltpu.SemaphoreType.DMA
     whole = jax.ShapeDtypeStruct((8, SB, 1024), F32)
     return pl.pallas_call(
-        named_kernel,
+        functools.partial(named_kernel, room),
         out_shape=[
             jax.ShapeDtypeStruct((1024, 1024), F32),
             jax.ShapeDtypeStruct((4, 8, SB, SB), F32),
             jax.ShapeDtypeStruct((8, 8, SB, SB), F32),
-            jax.ShapeDtypeStruct((8, SLOTS, SB, SB), F32),
+            jax.ShapeDtypeStruct((8, room, SB, SB), F32),
             whole,
             whole,
             whole,
@@ -635,12 +640,12 @@
             pltpu.VMEM((1024, 1024), F32),
             pltpu.VMEM((3, 128, SB), jnp.int32),
             pltpu.VMEM((3, 64, SB), jnp.int32),
-            pltpu.VMEM((2, 16 + SLOTS, SB, SB), F32),
-            pltpu.VMEM((16 + SLOTS, 2 * SB, SB), BF16),
+            pltpu.VMEM((2, 16 + room, SB, SB), F32),
+            pltpu.VMEM((16 + room, 2 * SB, SB), BF16),
             pltpu.VMEM((16, SB, SB), F32),
-            pltpu.VMEM((8, SLOTS, SB, SB), F32),
-            pltpu.VMEM((8, SLOTS, SB, SB), F32),
-            *[pltpu.VMEM((SLOTS, SB, SB), F32)] * 8,
+            pltpu.VMEM((8, room, SB, SB), F32),
+            pltpu.VMEM((8, room, SB, SB), F32),
+            *[pltpu.VMEM((room, SB, SB), F32)] * 8,
             pltpu.VMEM((8, 8, SB, SB), F32),
             pltpu.VMEM((4, 8, SB, SB), F32),
             pltpu.VMEM((2, 2, SB, 1024), F32),
@@ -651,9 +656,9 @@
             pltpu.VMEM((8, SB, SB), F32),
             pltpu.SMEM((4, 48), jnp.int32),
             pltpu.SMEM((4, 48), F32),
-            pltpu.SMEM((4, 3 * SLOTS), jnp.int32),
-            pltpu.SMEM((4, 3 * SLOTS), F32),
-            pltpu.SMEM((4, 2 * SLOTS), jnp.int32),
+            pltpu.SMEM((4, 3 * room), jnp.int32),
+            pltpu.SMEM((4, 3 * room), F32),
+            pltpu.SMEM((4, 2 * room), jnp.int32),
             dma((4, 8)),
             dma((4, 8)),
             dma((4, 2, 2)),
@@ -661,9 +666,9 @@
             dma((4, 5)),
         ],
         compiler_params=pltpu.CompilerParams(
-            collective_id=0, has_side_effects=True, vmem_limit_bytes=109 * 2**19
+            collective_id=ROOMS.index(room), has_side_effects=True, vmem_limit_bytes=109 * 2**19
         ),
-        name="named_sigma",
+        name=f"named_sigma_{room}",
     )(
         coef.reshape(8, SB, 1024),
         asrc,
@@ -1164,7 +1169,7 @@
             dma((8,)),
         ],
         compiler_params=pltpu.CompilerParams(
-            collective_id=1, has_side_effects=True, vmem_limit_bytes=109 * 2**19
+            collective_id=len(ROOMS), has_side_effects=True, vmem_limit_bytes=109 * 2**19
         ),
         name="any_couplings",
     )(coef, asrc, apair, alinks, bsrc, bpair, blinks, one_body)[0]
@@ -1190,17 +1195,20 @@
         beta_pair.T,
         beta_links.transpose(1, 0, 2),
     )
-    slots, fits = message_tables(tables[0])
-
-    def with_slots():
-        return named_sigma(coefficients, alpha_energy, beta_energy, one_body, *tables, slots)
+    slots, choice = message_tables(tables[0])
+
+    def with_slots(room):
+        return tuple(
+            named_sigma(room, coefficients, alpha_energy, beta_energy, one_body, *tables, slots)
+        )
 
     def without_slots():
         terms = any_couplings(coefficients, one_body, *tables)
         diagonal = (alpha_energy[:, None] + beta_energy[None, :]) * coefficients
         return diagonal + terms, jnp.zeros((4, 8, SB, SB), F32)
 
-    return finish_sigma(*lax.cond(fits[0, 0] == 1, lambda: tuple(with_slots()), without_slots))
+    branches = [functools.partial(with_slots, room) for room in ROOMS] + [without_slots]
+    return finish_sigma(*lax.switch(choice[0, 0], branches))
 
 
 def solution(mesh):

time: 133 us -> 134 us (level)
  no operation moved by 1% of the time
where the time goes in v5:
time: 134 us; the launch traced here: 133 us
  Pallas kernels  132 us (99%)
    pallas_call x1, Pallas kernels, named_sigma(): pl.pallas_call(functools.partial(named_kernel, room), out_shape=[jax.Shap...  128 us

profile of v5, /device:TPU:0, one launch (start us, length us, event | category | flops | bytes accessed | tf_op | source)
XLA Modules:
  0.0 133.2 jit_solution(5040940858338648906)
XLA Ops:
  0.0 1.5 %message_tables.1 = (s32[2,8,128]{2,1,0:T(8,128)S(1)}, s32[1,1]{1,0:T(1,128)}) custom-call(s32[3,128]{1,0:T(4,128)} %bitcast.25), custom_call_target="tpu_custom_call" | custom-call | tf_op jit(solution)/shard_map/message_tables/pallas_call | solution.py:96
  2.2 128.7 %conditional.1 = (f32[1024,1024]{1,0:T(8,128)S(1)}, f32[4,8,128,128]{3,2,1,0:T(8,128)S(1)}) conditional(s32[]{:T(128)} %bitcast.7, (f32[1024,1024]{1,0:T(8,128)}, f32[1024]{0:T(1024)}, f32[1024]{0:T(1024)}, s32[3,128]{1,0:T(4,128)}, s32[3,128]{1,0:T(4,128)}, /*index=5*/s32[3,128,128]{2,1,0:T(8,128)}, s32[3,64]{1,0:T(4,128)}, ...), branch_computations={%region_0.0_spmd, %region_1.0_spmd, %region_2.0_spmd} | conditional | flops 3145728 | bytes 31498344 | solution.py:1211
  2.4 128.0 %named_sigma_13.1 = (f32[1024,1024]{1,0:T(8,128)S(1)}, f32[4,8,128,128]{3,2,1,0:T(8,128)S(1)}, f32[8,8,128,128]{3,2,1,0:T(8,128)}, f32[8,13,128,128]{3,2,1,0:T(8...) custom-call(f32[8,128,1024]{2,1,0:T(8,128)} %bitcast.14, ...), custom_call_target="tpu_custom_call" | custom-call | tf_op jit(solution)/shard_map/cond/branch_1_fun/named_sigma_13/pallas_call | solution.py:625
  130.9 2.0 %finish_sigma.1 = f32[1024,1024]{1,0:T(8,128)} custom-call(f32[1024,1024]{1,0:T(8,128)S(1)} %get-tuple-element.112.part, f32[4,8,128,128]{3,2,1,0:T(8,128)S(1)} %get-tuple-element.113.tail), custom_call_target="tpu_custom_call" | custom-call | tf_op jit(solution)/shard_map/finish_sigma/pallas_call | solution.py:704
